TPU v7x, 256 devices: a whole 4x4x8 slice. The times are simulated.
256 devices in a mesh: tile: 16 (over x, y_hi, core), trac: 16 (over y_lo, z).
Axes of the slice: x: 4, y: 4 (y_hi: 2, y_lo: 2; y = y_hi * 2 + y_lo), z: 8, core: 2. Of those that a mesh axis runs over, the one named last changes fastest.
Arguments:
- tracers: float32 [128, 4096, 128], P(None, ('tile', 'trac')), may hold values from -6 to 6
- winds: float32 [2, 4096, 128], P(None, ('tile', 'trac')), may hold values from -4 to 4
- chem_linear: float32 [128, 128], replicated, may hold values from -0.5 to 0.5
- chem_loss: float32 [128], replicated, may hold values from 0.5 to 4
- chem_left: float32 [4, 128, 128], replicated, may hold values from -0.25 to 0.25
- chem_right: float32 [4, 128, 128], replicated, may hold values from -0.25 to 0.25
- active_cells: int32 [256], P(('tile', 'trac')), may hold values from 256 to 2048
Outputs:
- tracers_out: float32 [128, 4096, 128], P(None, ('tile', 'trac'))
- winds_out: float32 [2, 4096, 128], P(None, ('tile', 'trac'))
Inputs may be any that keep to these rules, and one draw needn't show every extreme that they name: `active_cells`: active cells are the leading ones of the tile in row-major order.
All inputs are finite; a program needn't handle non-finite values.
Results may differ from a plain program's by a relative error of at most 0.0003.
Values sent between devices are 32-bit elements; how exact they have to be, the bound alone decides.
No kernel may reach another device: no remote copies, remote signals or barrier semaphores. Data moves between devices by JAX's collectives and lax.ppermute only.
A program may use at most 64 MiB of HBM per device.

v0:
```python
import functools

import jax
import jax.numpy as jnp
from jax import lax
from jax.experimental import pallas as pl
from jax.experimental.pallas import tpu as pltpu
from jax.sharding import PartitionSpec as P

SUBS = 4
CHEM_STEPS = 3
PAIRS = 4
DT_WIND = 0.1
VISCOSITY = 0.2
DT_TRACER = 0.1
DT_CHEM = 0.1

S = 128
R = 16
C = 128
OUTS = S * (1 + 2 * PAIRS)
F32 = jnp.float32
BF16 = jnp.bfloat16
VMEM_LIMIT = 48 * 1024 * 1024


def lanes(x, shift):
    return pltpu.roll(x, shift % C, 1)


def rows_rolled(x, shift):
    return pltpu.roll(x, shift % x.shape[0], 0)


def pack_kernel(x_ref, up_ref, down_ref):
    for r in range(SUBS):
        for g in range(S // 8):
            up_ref[pl.ds(r * S + 8 * g, 8), :] = x_ref[pl.ds(8 * g * R + R - SUBS + r, 8, stride=R), :]
            down_ref[pl.ds(r * S + 8 * g, 8), :] = x_ref[pl.ds(8 * g * R + r, 8, stride=R), :]


def weights_kernel(linear_ref, loss_ref, left_ref, right_ref, w_ref):
    row = lax.broadcasted_iota(jnp.int32, (S, S), 0)
    col = lax.broadcasted_iota(jnp.int32, (S, S), 1)
    diagonal = jnp.where(row == col, jnp.broadcast_to(loss_ref[...], (S, S)), 0.0)
    parts = [linear_ref[...] - diagonal]
    for p in range(PAIRS):
        parts += [left_ref[p], right_ref[p]]
    for i, part in enumerate(parts):
        hi = part.astype(BF16)
        lo = (part - hi.astype(F32)).astype(BF16)
        w_ref[pl.ds(i * S, S), pl.ds(0, S)] = hi
        w_ref[pl.ds(i * S, S), pl.ds(S, S)] = hi
        w_ref[pl.ds(i * S, S), pl.ds(2 * S, S)] = lo
        w_ref[pl.ds(i * S, S), pl.ds(3 * S, S)] = lo


def tendency(u, v):
    out = []
    for f in (u, v):
        east, west, north, south = lanes(f, -1), lanes(f, 1), rows_rolled(f, -1), rows_rolled(f, 1)
        along = (east - west) * 0.5
        across = (north - south) * 0.5
        spread = east + west + north + south - 4.0 * f
        out.append(-(u * along + v * across) + VISCOSITY * spread)
    return out


def wind_step(u, v):
    du, dv = tendency(u, v)
    fu, fv = u + DT_WIND * du, v + DT_WIND * dv
    du, dv = tendency(fu, fv)
    su = 0.75 * u + 0.25 * (fu + DT_WIND * du)
    sv = 0.75 * v + 0.25 * (fv + DT_WIND * dv)
    du, dv = tendency(su, sv)
    return (
        u / 3.0 + 2.0 / 3.0 * (su + DT_WIND * du),
        v / 3.0 + 2.0 / 3.0 * (sv + DT_WIND * dv),
    )


def coefficients(u, v, coef_ref):
    coef_ref[0] = 1.0 - DT_TRACER * (jnp.abs(u) + jnp.abs(v))
    coef_ref[1] = -DT_TRACER * lanes(jnp.minimum(u, 0.0), -1)
    coef_ref[2] = DT_TRACER * lanes(jnp.maximum(u, 0.0), 1)
    coef_ref[3] = -DT_TRACER * rows_rolled(jnp.minimum(v, 0.0), -1)
    coef_ref[4] = DT_TRACER * rows_rolled(jnp.maximum(v, 0.0), 1)


def spread_rows(coef_ref, wide_ref, rows):
    for k in range(5):
        for r in rows:
            wide_ref[k, r] = jnp.broadcast_to(coef_ref[k, pl.ds(r, 1), :], (8, C))


def subcycles(groups, wide_ref, first):
    for sub in range(SUBS):
        size = len(groups[0])
        done = [[] for _ in groups]
        for i in range(1, size - 1):
            k = [wide_ref[j, first + sub + i] for j in range(5)]
            for q, d in zip(groups, done):
                d.append(
                    k[0] * q[i]
                    + k[1] * lanes(q[i], -1)
                    + k[2] * lanes(q[i], 1)
                    + (k[3] * q[i + 1] + k[4] * q[i - 1])
                )
        groups = done
    return groups


def react(conc, scale, w_ref):
    for _ in range(CHEM_STEPS):
        hi = conc.astype(BF16)
        lo = (conc - hi.astype(F32)).astype(BF16)
        both = jnp.concatenate([hi, lo, hi, lo], axis=0)
        y = jnp.dot(w_ref[...], both, preferred_element_type=F32)
        rate = y[0:S]
        for p in range(PAIRS):
            at = (1 + 2 * p) * S
            rate = rate + y[at : at + S] * y[at + S : at + 2 * S]
        conc = conc + rate * scale
    return conc


def scale_of(rows, count):
    col = lax.broadcasted_iota(jnp.int32, (1, C), 1)
    parts = [jnp.where(col + r * C < count, DT_CHEM, 0.0).astype(F32) for r in rows]
    return jnp.concatenate(parts, axis=1)


TOGETHER = 2


def inner_kernel(
    count_ref, x_ref, winds_ref, below_ref, above_ref, w_ref,
    inner_ref, winds_out_ref, wide_winds_ref, coef_ref, wide_ref, conc_ref,
):
    field = [
        jnp.concatenate([below_ref[k, 8:16, :], winds_ref[k], above_ref[k, 0:8, :]], axis=0)
        for k in range(2)
    ]
    u, v = wind_step(*field)
    winds_out_ref[0] = u[8:24]
    winds_out_ref[1] = v[8:24]
    wide_winds_ref[0] = u
    wide_winds_ref[1] = v
    coefficients(u, v, coef_ref)
    spread_rows(coef_ref, wide_ref, range(8 + 1, 8 + R - 1))

    def some_groups(step, carry):
        groups = []
        for k in range(TOGETHER):
            at = (step * TOGETHER + k) * (8 * R)
            groups.append([x_ref[pl.ds(at + r, 8, stride=R), :] for r in range(R)])
        done = subcycles(groups, wide_ref, 8)
        for k in range(TOGETHER):
            at = pl.multiple_of((step * TOGETHER + k) * 8, 8)
            for i, q in enumerate(done[k]):
                conc_ref[i, pl.ds(at, 8), :] = q
        return carry

    lax.fori_loop(0, S // 8 // TOGETHER, some_groups, 0)
    count = count_ref[0]
    for b in range((R - 2 * SUBS) // 2):
        conc = jnp.concatenate([conc_ref[2 * b], conc_ref[2 * b + 1]], axis=1)
        conc = react(conc, scale_of([SUBS + 2 * b, SUBS + 2 * b + 1], count), w_ref)
        inner_ref[2 * b] = conc[:, :C]
        inner_ref[2 * b + 1] = conc[:, C:]


def edge_kernel(
    count_ref, x_ref, below_ref, above_ref, wide_winds_ref, w_ref, inner_ref,
    out_ref, coef_ref, wide_ref, conc_ref,
):
    coefficients(wide_winds_ref[0], wide_winds_ref[1], coef_ref)
    spread_rows(coef_ref, wide_ref, list(range(8 - SUBS + 1, 8 + 2 * SUBS - 1)))
    spread_rows(coef_ref, wide_ref, list(range(8 + R - 2 * SUBS + 1, 8 + R + SUBS - 1)))

    def some_groups(step, carry):
        for side in range(2):
            groups = []
            for k in range(TOGETHER):
                g = step * TOGETHER + k
                own = [
                    x_ref[pl.ds(g * (8 * R) + r + side * (R - 2 * SUBS), 8, stride=R), :]
                    for r in range(2 * SUBS)
                ]
                far_ref = above_ref if side else below_ref
                far = [far_ref[pl.ds(pl.multiple_of(r * S + g * 8, 8), 8), :] for r in range(SUBS)]
                groups.append(own + far if side else far + own)
            done = subcycles(groups, wide_ref, 8 + R - 2 * SUBS if side else 8 - SUBS)
            for k in range(TOGETHER):
                at = pl.multiple_of((step * TOGETHER + k) * 8, 8)
                for i, q in enumerate(done[k]):
                    conc_ref[side * SUBS + i, pl.ds(at, 8), :] = q
        return carry

    lax.fori_loop(0, S // 8 // TOGETHER, some_groups, 0)
    for r in range(R - 2 * SUBS):
        for g in range(S // 8):
            out_ref[pl.ds(8 * g * R + SUBS + r, 8, stride=R), :] = inner_ref[r, pl.ds(8 * g, 8), :]
    count = count_ref[0]
    for b in range(SUBS):
        pair = [r if r < SUBS else R - 2 * SUBS + r for r in (2 * b, 2 * b + 1)]
        conc = jnp.concatenate([conc_ref[2 * b], conc_ref[2 * b + 1]], axis=1)
        conc = react(conc, scale_of(pair, count), w_ref)
        for j, r in enumerate(pair):
            for g in range(S // 8):
                out_ref[pl.ds(8 * g * R + r, 8, stride=R), :] = conc[8 * g : 8 * g + 8, j * C : (j + 1) * C]


def kernel_call(kernel, outs, scratch=(), scalars=0, operands=0):
    vmem = pl.BlockSpec(memory_space=pltpu.VMEM)
    smem = pl.BlockSpec(memory_space=pltpu.SMEM)
    return pl.pallas_call(
        kernel,
        out_shape=[jax.ShapeDtypeStruct(shape, dtype) for shape, dtype in outs],
        in_specs=[smem] * scalars + [vmem] * operands,
        out_specs=[vmem] * len(outs),
        scratch_shapes=[pltpu.VMEM(shape, F32) for shape in scratch],
        compiler_params=pltpu.CompilerParams(vmem_limit_bytes=VMEM_LIMIT),
    )


def on_device(tracers, winds, linear, loss, left, right, active):
    axes = ("tile", "trac")
    size = lax.axis_size(axes)
    up = [(i, (i + 1) % size) for i in range(size)]
    down = [(b, a) for a, b in up]

    winds_below = lax.ppermute(winds, axes, up)
    winds_above = lax.ppermute(winds, axes, down)
    x = tracers.reshape(S * R, C)
    edge = ((SUBS * S, C), F32)
    last, leading = kernel_call(pack_kernel, [edge, edge], operands=1)(x)
    below = lax.ppermute(last, axes, up)
    above = lax.ppermute(leading, axes, down)
    (w,) = kernel_call(weights_kernel, [((OUTS, 4 * S), BF16)], operands=4)(
        linear, loss.reshape(1, S), left, right
    )
    rows = R - 2 * SUBS
    tables = [(5, 32, C), (5, 32, 8, C), (rows, S, C)]
    inner, winds_new, wide_winds = kernel_call(
        inner_kernel,
        [((rows, S, C), F32), ((2, R, C), F32), ((2, 32, C), F32)],
        tables, scalars=1, operands=5,
    )(active, x, winds, winds_below, winds_above, w)
    (out,) = kernel_call(edge_kernel, [((S * R, C), F32)], tables, scalars=1, operands=6)(
        active, x, below, above, wide_winds, w, inner
    )
    return out.reshape(S, R, C), winds_new


def solution(mesh):
    grid = P(None, ("tile", "trac"), None)
    return jax.shard_map(
        on_device,
        mesh=mesh,
        in_specs=(grid, grid, P(), P(), P(), P(), P(("tile", "trac"))),
        out_specs=(grid, grid),
        check_vma=False,
    )
```

profile of v0, /device:TPU:0, one launch (start us, length us, event | category | flops | bytes accessed | tf_op | source)
XLA Modules:
  0.0 43.8 jit_solution(10479297483187222898)
XLA Ops:
  0.6 0.0 copy-start
  0.6 1.2 %copy-done = f32[128,16,128]{2,1,0:T(8,128)S(1)} copy-done((f32[128,16,128]{2,1,0:T(8,128)S(1)}, f32[128,16,128]{2,1,0:T(8,128)}, u32[]{:S(2)}) %copy-start) | copy-done | bytes 1048600
  1.9 0.0 copy-start.1
  1.9 0.2 shard_map.86
  2.0 0.3 collective-permute-start
  2.3 8.1 %collective-permute-start.1 = (f32[512,128]{1,0:T(8,128)S(1)}, f32[512,128]{1,0:T(8,128)S(1)}, u32[]{:S(2)}, u32[]{:S(2)}) collective-permute-start(f32[512,128]{1,0:T(8,128)S(1)} %get-tuple-element.8), channel_id=1, source_target_pairs={{1,0},{2,1},{3,2},{4,3},{5,4},{6,5},{7,6},{8,7},{9,8},{10,9},{11,1... | collective-permute-start | bytes 786440 | tf_op jit(solution)/shard_map/ppermute | solution.py:239
  10.4 0.0 collective-permute-start.2
  10.4 7.2 %collective-permute-start.3 = (f32[2,16,128]{2,1,0:T(8,128)}, f32[2,16,128]{2,1,0:T(8,128)S(1)}, u32[]{:S(2)}, u32[]{:S(2)}) collective-permute-start(f32[2,16,128]{2,1,0:T(8,128)} %winds_ref.1), channel_id=1, source_target_pairs={{1,0},{2,1},{3,2},{4,3},{5,4},{6,5},{7,6},{8,7},{9,8},{10,9},{11,1... | collective-permute-start | bytes 49160 | tf_op jit(solution)/shard_map/ppermute | solution.py:234
  18.2 0.0 copy-start.2
  18.3 0.9 %copy-done.2 = f32[4,128,128]{2,1,0:T(8,128)S(1)} copy-done((f32[4,128,128]{2,1,0:T(8,128)S(1)}, f32[4,128,128]{2,1,0:T(8,128)}, u32[]{:S(2)}) %copy-start.2) | copy-done | bytes 262168
  19.2 0.0 copy-start.3
  19.2 0.9 %copy-done.3 = f32[4,128,128]{2,1,0:T(8,128)S(1)} copy-done((f32[4,128,128]{2,1,0:T(8,128)S(1)}, f32[4,128,128]{2,1,0:T(8,128)}, u32[]{:S(2)}) %copy-start.3) | copy-done | bytes 262168
  20.1 0.0 copy-start.4
  20.1 0.8 %copy-done.4 = f32[128,128]{1,0:T(8,128)S(1)} copy-done((f32[128,128]{1,0:T(8,128)S(1)}, f32[128,128]{1,0:T(8,128)}, u32[]{:S(2)}) %copy-start.4) | copy-done | bytes 65560
  21.0 0.7 %copy-done.6 = f32[128]{0:T(128)S(1)} copy-done((f32[128]{0:T(128)S(1)}, f32[128]{0:T(128)}, u32[]{:S(2)}) %copy-start.6) | copy-done | bytes 536
  21.6 0.2 shard_map.87.w_ref
  21.8 0.0 collective-permute-done.2.below_ref
  21.8 0.0 collective-permute-done.3.above_ref
  21.8 0.0 copy-done.1
  21.8 0.5 %copy-done.5 = f32[2,16,128]{2,1,0:T(8,128)S(1)} copy-done((f32[2,16,128]{2,1,0:T(8,128)S(1)}, f32[2,16,128]{2,1,0:T(8,128)}, u32[]{:S(2)}) %copy-start.5) | copy-done | bytes 16408
  22.4 10.2 %shard_map.88 = (f32[8,128,128]{2,1,0:T(8,128)S(1)}, f32[2,16,128]{2,1,0:T(8,128)}, f32[2,32,128]{2,1,0:T(8,128)S(1)}) custom-call(s32[1]{0:T(128)S(6)} %copy.9.count_ref, f32[2048,128]{1,0:T(8,128)S(1)} %bitcast.4, f32[2,16,128]{2,1,0:T(8,128)S(1)} %copy-done.5, f32[2,16,128]{2,1,0:T(8,128)S(1)} %collective-permute-done.2.below_ref, ...), custom_call_target="tpu_custom_call" | custom-call | tf_op jit(solution)/shard_map/pallas_call | solution.py:245
  32.6 0.0 collective-permute-done.below_ref
  32.6 0.0 collective-permute-done.1.above_ref
  32.6 11.2 %shard_map.89 = f32[2048,128]{1,0:T(8,128)} custom-call(s32[1]{0:T(128)S(6)} %copy.9.count_ref, f32[2048,128]{1,0:T(8,128)S(1)} %bitcast.5, f32[512,128]{1,0:T(8,128)S(1)} %collective-permute-done.below_ref, f32[512,128]{1,0:T(8,128)S(1)} %collective-permute-done.1.above_ref, f32[2,32,128]{2,1,0:T(8,128)S(1)} %get-tuple-element.9.wide_winds_ref, ...), custom_call_target="tpu_custom_call" | custom-call | tf_op jit(solution)/shard_map/pallas_call | solution.py:250
  (2 shorter events, 0.0 us)
Async XLA Ops:
  0.6 1.2 %copy-start = (f32[128,16,128]{2,1,0:T(8,128)S(1)}, f32[128,16,128]{2,1,0:T(8,128)}, u32[]{:S(2)}) copy-start(f32[128,16,128]{2,1,0:T(8,128)} %param.7) | copy-start | bytes 3145732
  1.9 20.0 %copy-start.1 = (f32[128,16,128]{2,1,0:T(8,128)S(1)}, f32[128,16,128]{2,1,0:T(8,128)}, u32[]{:S(2)}) copy-start(f32[128,16,128]{2,1,0:T(8,128)} %param.7) | copy-start | bytes 3145732
  2.0 30.6 %collective-permute-start = (f32[512,128]{1,0:T(8,128)S(1)}, f32[512,128]{1,0:T(8,128)S(1)}, u32[]{:S(2)}, u32[]{:S(2)}) collective-permute-start(f32[512,128]{1,0:T(8,128)S(1)} %get-tuple-element.7), channel_id=1, source_target_pairs={{0,1},{1,2},{2,3},{3,4},{4,5},{5,6},{6,7},{7,8},{8,9},{9,10},{10,1... | collective-permute-start | bytes 786440 | tf_op jit(solution)/shard_map/ppermute | solution.py:238
  2.3 30.3 %collective-permute-start.1 = (f32[512,128]{1,0:T(8,128)S(1)}, f32[512,128]{1,0:T(8,128)S(1)}, u32[]{:S(2)}, u32[]{:S(2)}) collective-permute-start(f32[512,128]{1,0:T(8,128)S(1)} %get-tuple-element.8), channel_id=1, source_target_pairs={{1,0},{2,1},{3,2},{4,3},{5,4},{6,5},{7,6},{8,7},{9,8},{10,9},{11,1... | collective-permute-start | bytes 786440 | tf_op jit(solution)/shard_map/ppermute | solution.py:239
  10.4 11.4 %collective-permute-start.2 = (f32[2,16,128]{2,1,0:T(8,128)}, f32[2,16,128]{2,1,0:T(8,128)S(1)}, u32[]{:S(2)}, u32[]{:S(2)}) collective-permute-start(f32[2,16,128]{2,1,0:T(8,128)} %winds_ref.1), channel_id=1, source_target_pairs={{0,1},{1,2},{2,3},{3,4},{4,5},{5,6},{6,7},{7,8},{8,9},{9,10},{10,1... | collective-permute-start | bytes 49160 | tf_op jit(solution)/shard_map/ppermute | solution.py:233
  10.4 11.4 %collective-permute-start.3 = (f32[2,16,128]{2,1,0:T(8,128)}, f32[2,16,128]{2,1,0:T(8,128)S(1)}, u32[]{:S(2)}, u32[]{:S(2)}) collective-permute-start(f32[2,16,128]{2,1,0:T(8,128)} %winds_ref.1), channel_id=1, source_target_pairs={{1,0},{2,1},{3,2},{4,3},{5,4},{6,5},{7,6},{8,7},{9,8},{10,9},{11,1... | collective-permute-start | bytes 49160 | tf_op jit(solution)/shard_map/ppermute | solution.py:234
  18.2 1.0 %copy-start.2 = (f32[4,128,128]{2,1,0:T(8,128)S(1)}, f32[4,128,128]{2,1,0:T(8,128)}, u32[]{:S(2)}) copy-start(f32[4,128,128]{2,1,0:T(8,128)} %left_ref.1) | copy-start | bytes 786436
  19.2 0.9 %copy-start.3 = (f32[4,128,128]{2,1,0:T(8,128)S(1)}, f32[4,128,128]{2,1,0:T(8,128)}, u32[]{:S(2)}) copy-start(f32[4,128,128]{2,1,0:T(8,128)} %right_ref.1) | copy-start | bytes 786436
  20.1 0.8 %copy-start.4 = (f32[128,128]{1,0:T(8,128)S(1)}, f32[128,128]{1,0:T(8,128)}, u32[]{:S(2)}) copy-start(f32[128,128]{1,0:T(8,128)} %linear_ref.1) | copy-start | bytes 196612
  21.0 0.7 %copy-start.6 = (f32[128]{0:T(128)S(1)}, f32[128]{0:T(128)}, u32[]{:S(2)}) copy-start(f32[128]{0:T(128)} %param.10) | copy-start | bytes 1540
  21.6 0.7 %copy-start.5 = (f32[2,16,128]{2,1,0:T(8,128)S(1)}, f32[2,16,128]{2,1,0:T(8,128)}, u32[]{:S(2)}) copy-start(f32[2,16,128]{2,1,0:T(8,128)} %winds_ref.1) | copy-start | bytes 49156
where the time goes:
time: 44.1 us; the launch traced here: 43.8 us
  Pallas kernels  21.8 us (49%)
  starting transfers between devices  15.6 us (35%)
  local copies, waits for them, and re-layouts  5.13 us (12%)
  between operations  1.34 us (3%)
    pallas_call x1, Pallas kernels, on_device(): kernel_call(edge_kernel, [((S * R, C), F32)], tables, scalars=1, operands=6)  11.2 us
    pallas_call x1, Pallas kernels, on_device(): kernel_call(inner_kernel, [((rows, S, C), F32), ((2, R, C), F32), ((2, 32...  10.2 us
    ppermute x1, starting transfers between devices, on_device(): above = lax.ppermute(leading, axes, down)  8.12 us
    ppermute x1, starting transfers between devices, on_device(): winds_above = lax.ppermute(winds, axes, down)  7.17 us
    unnamed x14, local copies, waits for them, and re-layouts  5.13 us
  transfers between devices with their start and end apart: 4, of which 0 were waited for; matrix products, arithmetic and copies ran while one was open for 0% of the time, Pallas kernels for 24%

commit v1 on v0

v1 whole, which is shorter than its diff:
```python
import functools

import jax
import jax.numpy as jnp
from jax import lax
from jax.experimental import pallas as pl
from jax.experimental.pallas import tpu as pltpu
from jax.sharding import PartitionSpec as P

SUBS = 4
CHEM_STEPS = 3
PAIRS = 4
DT_WIND = 0.1
VISCOSITY = 0.2
DT_TRACER = 0.1
DT_CHEM = 0.1

AXES = ("tile", "trac")
S = 128
R = 16
C = 128
OUTS = S * (1 + 2 * PAIRS)
F32 = jnp.float32
BF16 = jnp.bfloat16
VMEM_LIMIT = 48 * 1024 * 1024


def lanes(x, shift):
    return pltpu.roll(x, shift % C, 1)


def rows_rolled(x, shift):
    return pltpu.roll(x, shift % x.shape[0], 0)


def is_even():
    return 1 - lax.axis_index(AXES) % 2


def pack_kernel(
    x_hbm, winds_hbm, linear_hbm, loss_hbm, left_hbm, right_hbm,
    near_ref, far_ref, x_ref, winds_ref, raw_ref, loss_ref, sems,
):
    even = is_even()
    moves = []
    for k in range(CHUNKS):
        part = pl.ds(k * (S * R // CHUNKS), S * R // CHUNKS)
        moves.append((x_hbm.at[part], x_ref.at[part]))
    moves.append((winds_hbm, winds_ref))
    moves.append((left_hbm, raw_ref.at[pl.ds(1, PAIRS)]))
    moves.append((right_hbm, raw_ref.at[pl.ds(1 + PAIRS, PAIRS)]))
    moves.append((linear_hbm, raw_ref.at[0]))
    moves.append((loss_hbm, loss_ref))
    copies = [pltpu.make_async_copy(a, b, sems.at[i]) for i, (a, b) in enumerate(moves)]
    for copy in copies:
        copy.start()
    for k in range(CHUNKS):
        copies[k].wait()
        for ref, side in ((near_ref, even), (far_ref, 1 - even)):
            for r in range(SUBS):
                for g in range(k * S // 8 // CHUNKS, (k + 1) * S // 8 // CHUNKS):
                    at = 8 * g * R + r + side * (R - SUBS)
                    ref[pl.ds(r * S + 8 * g, 8), :] = x_ref[pl.ds(at, 8, stride=R), :]
    copies[CHUNKS].wait()
    for ref, side in ((near_ref, even), (far_ref, 1 - even)):
        for k in range(2):
            ref[pl.ds(SUBS * S + 8 * k, 8), :] = winds_ref[k, pl.ds(pl.multiple_of(side * 8, 8), 8), :]
    for copy in copies[CHUNKS + 1 :]:
        copy.wait()


def weights_kernel(raw_ref, loss_ref, w_ref):
    row = lax.broadcasted_iota(jnp.int32, (S, S), 0)
    col = lax.broadcasted_iota(jnp.int32, (S, S), 1)
    diagonal = jnp.where(row == col, jnp.broadcast_to(loss_ref[...], (S, S)), 0.0)
    parts = [raw_ref[0] - diagonal]
    for p in range(PAIRS):
        parts += [raw_ref[1 + p], raw_ref[1 + PAIRS + p]]
    for i, part in enumerate(parts):
        hi = part.astype(BF16)
        lo = (part - hi.astype(F32)).astype(BF16)
        w_ref[pl.ds(i * S, S), pl.ds(0, S)] = hi
        w_ref[pl.ds(i * S, S), pl.ds(S, S)] = hi
        w_ref[pl.ds(i * S, S), pl.ds(2 * S, S)] = lo
        w_ref[pl.ds(i * S, S), pl.ds(3 * S, S)] = lo


def tendency(u, v):
    out = []
    for f in (u, v):
        east, west, north, south = lanes(f, -1), lanes(f, 1), rows_rolled(f, -1), rows_rolled(f, 1)
        along = (east - west) * 0.5
        across = (north - south) * 0.5
        spread = east + west + north + south - 4.0 * f
        out.append(-(u * along + v * across) + VISCOSITY * spread)
    return out


def wind_step(u, v):
    du, dv = tendency(u, v)
    fu, fv = u + DT_WIND * du, v + DT_WIND * dv
    du, dv = tendency(fu, fv)
    su = 0.75 * u + 0.25 * (fu + DT_WIND * du)
    sv = 0.75 * v + 0.25 * (fv + DT_WIND * dv)
    du, dv = tendency(su, sv)
    return (
        u / 3.0 + 2.0 / 3.0 * (su + DT_WIND * du),
        v / 3.0 + 2.0 / 3.0 * (sv + DT_WIND * dv),
    )


def coefficients(u, v, wide_ref, rows):
    tables = [
        1.0 - DT_TRACER * (jnp.abs(u) + jnp.abs(v)),
        -DT_TRACER * lanes(jnp.minimum(u, 0.0), -1),
        DT_TRACER * lanes(jnp.maximum(u, 0.0), 1),
        -DT_TRACER * rows_rolled(jnp.minimum(v, 0.0), -1),
        DT_TRACER * rows_rolled(jnp.maximum(v, 0.0), 1),
    ]
    for k, table in enumerate(tables):
        for i, r in enumerate(rows):
            wide_ref[k, i] = jnp.broadcast_to(table[r : r + 1], (8, C))


def subcycles(groups, wide_ref):
    for sub in range(SUBS):
        size = len(groups[0])
        done = [[] for _ in groups]
        for i in range(1, size - 1):
            k = [wide_ref[j, sub + i - 1] for j in range(5)]
            for q, d in zip(groups, done):
                d.append(
                    k[0] * q[i]
                    + k[1] * lanes(q[i], -1)
                    + k[2] * lanes(q[i], 1)
                    + (k[3] * q[i + 1] + k[4] * q[i - 1])
                )
        groups = done
    return groups


def react(conc, scale, w_ref):
    for _ in range(CHEM_STEPS):
        hi = conc.astype(BF16)
        lo = (conc - hi.astype(F32)).astype(BF16)
        both = jnp.concatenate([hi, lo, hi, lo], axis=0)
        y = jnp.dot(w_ref[...], both, preferred_element_type=F32)
        rate = y[0:S]
        for p in range(PAIRS):
            at = (1 + 2 * p) * S
            rate = rate + y[at : at + S] * y[at + S : at + 2 * S]
        conc = conc + rate * scale
    return conc


TOGETHER = 2
CHUNKS = 4
H = R // 2


def half_kernel(last, *refs):
    (count_ref, x_ref, winds_ref, message_ref, w_ref, *rest) = refs
    if last:
        other_ref, _, out_hbm, winds_out_ref, wide_ref, conc_ref, stage_ref, sem = rest
    else:
        out_hbm, wide_ref, conc_ref, stage_ref, sem = rest
        other_ref = message_ref
    side = 1 - is_even() if last else is_even()
    high = side == 1
    field = []
    for k in range(2):
        here = message_ref[pl.ds(SUBS * S + 8 * k, 8), :]
        there = other_ref[pl.ds(SUBS * S + 8 * k, 8), :]
        field.append(
            jnp.concatenate([jnp.where(high, there, here), winds_ref[k], jnp.where(high, here, there)], axis=0)
        )
    u, v = wind_step(*field)
    if last:
        winds_out_ref[0] = u[8:24]
        winds_out_ref[1] = v[8:24]
    u, v = [jnp.where(high, f[8:32], f[0:24]) for f in (u, v)]
    coefficients(u, v, wide_ref, range(5, 5 + R - 2))

    def some_groups(step, carry):
        groups = []
        for k in range(TOGETHER):
            g = step * TOGETHER + k
            start = g * (8 * R)
            own = [x_ref[pl.ds(start + r + side * SUBS, 8, stride=R), :] for r in range(R - SUBS)]
            halo = [message_ref[pl.ds(pl.multiple_of(r * S + g * 8, 8), 8), :] for r in range(SUBS)]
            groups.append(
                [
                    jnp.where(
                        high,
                        own[i] if i < R - SUBS else halo[i - R + SUBS],
                        halo[i] if i < SUBS else own[i - SUBS],
                    )
                    for i in range(R)
                ]
            )
        done = subcycles(groups, wide_ref)
        for k in range(TOGETHER):
            at = pl.multiple_of((step * TOGETHER + k) * 8, 8)
            for i, q in enumerate(done[k]):
                conc_ref[i, pl.ds(at, 8), :] = q
        return carry

    lax.fori_loop(0, S // 8 // TOGETHER, some_groups, 0)
    conc = jnp.concatenate([conc_ref[i] for i in range(H)], axis=1)
    cell = lax.broadcasted_iota(jnp.int32, (1, H * C), 1) + side * (H * C)
    scale = jnp.where(cell < count_ref[0], DT_CHEM, 0.0).astype(F32)
    conc = react(conc, scale, w_ref)
    flat_ref = stage_ref.reshape(S * H, C)
    for i in range(H):
        for g in range(S // 8):
            flat_ref[pl.ds(8 * g * H + i, 8, stride=H), :] = conc[8 * g : 8 * g + 8, i * C : (i + 1) * C]
    copy = pltpu.make_async_copy(
        stage_ref, out_hbm.at[:, pl.ds(pl.multiple_of(side * H, H), H), :], sem
    )
    copy.start()
    copy.wait()


def on_device(tracers, winds, linear, loss, left, right, active):
    size = lax.axis_size(AXES)
    near = [(i, i ^ 1) for i in range(size)]
    far = [(i, (i + 1 if i % 2 else i - 1) % size) for i in range(size)]

    vmem = pl.BlockSpec(memory_space=pltpu.VMEM)
    smem = pl.BlockSpec(memory_space=pltpu.SMEM)
    hbm = pl.BlockSpec(memory_space=pltpu.HBM)
    params = pltpu.CompilerParams(vmem_limit_bytes=VMEM_LIMIT)
    message = jax.ShapeDtypeStruct((SUBS * S + 16, C), F32)
    to_near, to_far, x, winds, raw, loss = pl.pallas_call(
        pack_kernel,
        out_shape=[
            message,
            message,
            jax.ShapeDtypeStruct((S * R, C), F32),
            jax.ShapeDtypeStruct((2, R, C), F32),
            jax.ShapeDtypeStruct((1 + 2 * PAIRS, S, S), F32),
            jax.ShapeDtypeStruct((1, S), F32),
        ],
        in_specs=[hbm] * 6,
        out_specs=[vmem] * 6,
        scratch_shapes=[pltpu.SemaphoreType.DMA((CHUNKS + 5,))],
        compiler_params=params,
    )(
        *[
            pltpu.with_memory_space_constraint(a, pltpu.HBM)
            for a in (tracers.reshape(S * R, C), winds, linear, loss.reshape(1, S), left, right)
        ]
    )
    from_near = lax.ppermute(to_near, AXES, near)
    from_far = lax.ppermute(to_far, AXES, far)
    w = pl.pallas_call(
        weights_kernel,
        out_shape=jax.ShapeDtypeStruct((OUTS, 4 * S), BF16),
        in_specs=[vmem] * 2,
        out_specs=vmem,
        compiler_params=params,
    )(raw, loss)
    scratch = [
        pltpu.VMEM((5, R - 2, 8, C), F32),
        pltpu.VMEM((H, S, C), F32),
        pltpu.VMEM((S, H, C), F32),
        pltpu.SemaphoreType.DMA,
    ]
    whole = jax.ShapeDtypeStruct((S, R, C), F32)
    half = pl.pallas_call(
        functools.partial(half_kernel, False),
        out_shape=whole,
        in_specs=[smem] + [vmem] * 4,
        out_specs=hbm,
        scratch_shapes=scratch,
        compiler_params=params,
    )(active, x, winds, from_near, w)
    return pl.pallas_call(
        functools.partial(half_kernel, True),
        out_shape=[whole, jax.ShapeDtypeStruct((2, R, C), F32)],
        in_specs=[smem] + [vmem] * 5 + [hbm],
        out_specs=[hbm, vmem],
        scratch_shapes=scratch,
        input_output_aliases={6: 0},
        compiler_params=params,
    )(active, x, winds, from_far, w, from_near, half)


def solution(mesh):
    grid = P(None, ("tile", "trac"), None)
    return jax.shard_map(
        on_device,
        mesh=mesh,
        in_specs=(grid, grid, P(), P(), P(), P(), P(("tile", "trac"))),
        out_specs=(grid, grid),
        check_vma=False,
    )
```

time: 44.1 us -> 29.1 us (0.66)
  the two profiles are of different devices: /device:TPU:0 before, /device:TPU:1 now
where the time goes in v1:
time: 29.1 us; the launch traced here: 29 us
  Pallas kernels  18.5 us (64%)
  starting transfers between devices  9.07 us (31%)
  between operations  1.32 us (5%)
    pallas_call x1, Pallas kernels, on_device(): pl.pallas_call(functools.partial(half_kernel, True), out_shape=[whole, ja...  8.77 us
    pallas_call x1, Pallas kernels, on_device(): pl.pallas_call(functools.partial(half_kernel, False), out_shape=whole, in...  8.17 us
    ppermute x1, starting transfers between devices, on_device(): from_far = lax.ppermute(to_far, AXES, far)  6.52 us
    ppermute x1, starting transfers between devices, on_device(): from_near = lax.ppermute(to_near, AXES, near)  2.55 us
    pallas_call x1, Pallas kernels, on_device(): pl.pallas_call(pack_kernel, out_shape=[message, message, jax.ShapeDtypeSt...  1.45 us
  transfers between devices with their start and end apart: 2, of which 0 were waited for; matrix products, arithmetic and copies ran while one was open for 0% of the time, Pallas kernels for 29%

profile of v1, /device:TPU:1, one launch (start us, length us, event | category | flops | bytes accessed | tf_op | source)
XLA Modules:
  0.0 29.0 jit_solution(9186900834175484240)
XLA Ops:
  0.6 1.4 %shard_map.86 = (f32[528,128]{1,0:T(8,128)S(1)}, f32[528,128]{1,0:T(8,128)S(1)}, f32[2048,128]{1,0:T(8,128)S(1)}, f32[2,16,128]{2,1,0:T(8,128)S(1)}, f32[9,128,128]{2,1,0:T(8,128)S(1)}, /*index=5*/f32[1,128]{1,0:T(1,128)S(1)}) custom-call(f32[2048,128]{1,0:T(8,128)} %bitcast.2, f32[2,16,128]{2,1,0:T(8,128)} %winds_hbm.1, f32[128,128]{1,0:T(8,128)} %linear_hbm.1, ...), custom_call_target="tpu_custom_call" | custom-call | tf_op jit(solution)/shard_map/pallas_call | solution.py:234
  2.1 2.6 %collective-permute-start.1 = (f32[528,128]{1,0:T(8,128)S(1)}, f32[528,128]{1,0:T(8,128)S(1)}, u32[]{:S(2)}, u32[]{:S(2)}) collective-permute-start(f32[528,128]{1,0:T(8,128)S(1)} %get-tuple-element.13), channel_id=1, source_target_pairs={{0,1},{1,0},{2,3},{3,2},{4,5},{5,4},{6,7},{7,6},{8,9},{9,8},{10,11... | collective-permute-start | bytes 811016 | tf_op jit(solution)/shard_map/ppermute | solution.py:254
  4.6 6.5 %collective-permute-start = (f32[528,128]{1,0:T(8,128)S(1)}, f32[528,128]{1,0:T(8,128)S(1)}, u32[]{:S(2)}, u32[]{:S(2)}) collective-permute-start(f32[528,128]{1,0:T(8,128)S(1)} %get-tuple-element.10), channel_id=1, source_target_pairs={{0,255},{1,2},{2,1},{3,4},{4,3},{5,6},{6,5},{7,8},{8,7},{9,10},{10... | collective-permute-start | bytes 811016 | tf_op jit(solution)/shard_map/ppermute | solution.py:255
  11.8 0.2 shard_map.87.refs_4_
  12.0 0.0 collective-permute-done.1.refs_3_.refs_5_
  12.0 8.2 %shard_map.88.refs_6_ = f32[128,16,128]{2,1,0:T(8,128)} custom-call(s32[1]{0:T(128)S(6)} %copy.11.refs_0_, f32[2048,128]{1,0:T(8,128)S(1)} %get-tuple-element.8.refs_1_, f32[2,16,128]{2,1,0:T(8,128)S(1)} %get-tuple-element.9.refs_2_, f32[528,128]{1,0:T(8,128)S(1)} %collective-permute-done.1.refs_3_.refs_5_, bf16[1152,512]{1,0:T(8,128)(2,1)S(1)} %shard_map.87.refs_4_), custom_call_target="tpu_custom_call" | custom-call | tf_op jit(solution)/shard_map/pallas_call | solution.py:270
  20.2 0.0 collective-permute-done.refs_3_
  20.2 8.8 %shard_map.89 = (f32[128,16,128]{2,1,0:T(8,128)}, f32[2,16,128]{2,1,0:T(8,128)}) custom-call(s32[1]{0:T(128)S(6)} %copy.11.refs_0_, f32[2048,128]{1,0:T(8,128)S(1)} %get-tuple-element.8.refs_1_, f32[2,16,128]{2,1,0:T(8,128)S(1)} %get-tuple-element.9.refs_2_, f32[528,128]{1,0:T(8,128)S(1)} %collective-permute-done.refs_3_, ...), custom_call_target="tpu_custom_call", output_to_operand_aliasing={{0}: (6, {})} | custom-call | tf_op jit(solution)/shard_map/pallas_call | solution.py:278
Async XLA Ops:
  2.1 9.9 %collective-permute-start.1 = (f32[528,128]{1,0:T(8,128)S(1)}, f32[528,128]{1,0:T(8,128)S(1)}, u32[]{:S(2)}, u32[]{:S(2)}) collective-permute-start(f32[528,128]{1,0:T(8,128)S(1)} %get-tuple-element.13), channel_id=1, source_target_pairs={{0,1},{1,0},{2,3},{3,2},{4,5},{5,4},{6,7},{7,6},{8,9},{9,8},{10,11... | collective-permute-start | bytes 811016 | tf_op jit(solution)/shard_map/ppermute | solution.py:254
  4.6 15.5 %collective-permute-start = (f32[528,128]{1,0:T(8,128)S(1)}, f32[528,128]{1,0:T(8,128)S(1)}, u32[]{:S(2)}, u32[]{:S(2)}) collective-permute-start(f32[528,128]{1,0:T(8,128)S(1)} %get-tuple-element.10), channel_id=1, source_target_pairs={{0,255},{1,2},{2,1},{3,4},{4,3},{5,6},{6,5},{7,8},{8,7},{9,10},{10... | collective-permute-start | bytes 811016 | tf_op jit(solution)/shard_map/ppermute | solution.py:255

commit v2 on v1

--- a/solution.py
+++ b/solution.py
@@ -1,5 +1,3 @@
-import functools
-
 import jax
 import jax.numpy as jnp
 from jax import lax
@@ -69,7 +67,9 @@
         copy.wait()
 
 
-def weights_kernel(raw_ref, loss_ref, w_ref):
+def weights_kernel(count_ref, raw_ref, loss_ref, w_ref, scale_ref):
+    cell = lax.broadcasted_iota(jnp.int32, (1, R * C), 1)
+    scale_ref[...] = jnp.where(cell < count_ref[0], DT_CHEM, 0.0).astype(F32)
     row = lax.broadcasted_iota(jnp.int32, (S, S), 0)
     col = lax.broadcasted_iota(jnp.int32, (S, S), 1)
     diagonal = jnp.where(row == col, jnp.broadcast_to(loss_ref[...], (S, S)), 0.0)
@@ -122,103 +122,123 @@
             wide_ref[k, i] = jnp.broadcast_to(table[r : r + 1], (8, C))
 
 
-def subcycles(groups, wide_ref):
+def transport(groups, high, side, x_ref, message_ref, wide_ref, conc_ref):
+    states = []
+    for g in groups:
+        own = [x_ref[pl.ds(g * (8 * R) + r + side * SUBS, 8, stride=R), :] for r in range(R - SUBS)]
+        halo = [message_ref[pl.ds(r * S + g * 8, 8), :] for r in range(SUBS)]
+        states.append(
+            [
+                jnp.where(
+                    high,
+                    own[i] if i < R - SUBS else halo[i - R + SUBS],
+                    halo[i] if i < SUBS else own[i - SUBS],
+                )
+                for i in range(R)
+            ]
+        )
     for sub in range(SUBS):
-        size = len(groups[0])
-        done = [[] for _ in groups]
+        size = len(states[0])
+        done = [[] for _ in states]
         for i in range(1, size - 1):
             k = [wide_ref[j, sub + i - 1] for j in range(5)]
-            for q, d in zip(groups, done):
+            for q, d in zip(states, done):
                 d.append(
                     k[0] * q[i]
                     + k[1] * lanes(q[i], -1)
                     + k[2] * lanes(q[i], 1)
                     + (k[3] * q[i + 1] + k[4] * q[i - 1])
                 )
-        groups = done
-    return groups
+        states = done
+    for g, q in zip(groups, states):
+        for i in range(H):
+            conc_ref[i, pl.ds(8 * g, 8), :] = q[i]
 
 
 def react(conc, scale, w_ref):
-    for _ in range(CHEM_STEPS):
-        hi = conc.astype(BF16)
-        lo = (conc - hi.astype(F32)).astype(BF16)
-        both = jnp.concatenate([hi, lo, hi, lo], axis=0)
-        y = jnp.dot(w_ref[...], both, preferred_element_type=F32)
-        rate = y[0:S]
-        for p in range(PAIRS):
-            at = (1 + 2 * p) * S
-            rate = rate + y[at : at + S] * y[at + S : at + 2 * S]
-        conc = conc + rate * scale
-    return conc
-
-
-TOGETHER = 2
+    hi = conc.astype(BF16)
+    lo = (conc - hi.astype(F32)).astype(BF16)
+    both = jnp.concatenate([hi, lo, hi, lo], axis=0)
+    y = jnp.dot(w_ref[...], both, preferred_element_type=F32)
+    rate = y[0:S]
+    for p in range(PAIRS):
+        at = (1 + 2 * p) * S
+        rate = rate + y[at : at + S] * y[at + S : at + 2 * S]
+    return conc + rate * scale
+
+
 CHUNKS = 4
 H = R // 2
 
 
-def half_kernel(last, *refs):
-    (count_ref, x_ref, winds_ref, message_ref, w_ref, *rest) = refs
-    if last:
-        other_ref, _, out_hbm, winds_out_ref, wide_ref, conc_ref, stage_ref, sem = rest
-    else:
-        out_hbm, wide_ref, conc_ref, stage_ref, sem = rest
-        other_ref = message_ref
-    side = 1 - is_even() if last else is_even()
-    high = side == 1
-    field = []
-    for k in range(2):
-        here = message_ref[pl.ds(SUBS * S + 8 * k, 8), :]
-        there = other_ref[pl.ds(SUBS * S + 8 * k, 8), :]
-        field.append(
-            jnp.concatenate([jnp.where(high, there, here), winds_ref[k], jnp.where(high, here, there)], axis=0)
-        )
-    u, v = wind_step(*field)
-    if last:
-        winds_out_ref[0] = u[8:24]
-        winds_out_ref[1] = v[8:24]
+def new_winds(winds_ref, lower, upper):
+    return wind_step(
+        *[jnp.concatenate([lower[k * 8 : k * 8 + 8], winds_ref[k], upper[k * 8 : k * 8 + 8]], axis=0) for k in range(2)]
+    )
+
+
+def half_coefficients(u, v, high, wide_ref):
     u, v = [jnp.where(high, f[8:32], f[0:24]) for f in (u, v)]
     coefficients(u, v, wide_ref, range(5, 5 + R - 2))
 
-    def some_groups(step, carry):
-        groups = []
-        for k in range(TOGETHER):
-            g = step * TOGETHER + k
-            start = g * (8 * R)
-            own = [x_ref[pl.ds(start + r + side * SUBS, 8, stride=R), :] for r in range(R - SUBS)]
-            halo = [message_ref[pl.ds(pl.multiple_of(r * S + g * 8, 8), 8), :] for r in range(SUBS)]
-            groups.append(
-                [
-                    jnp.where(
-                        high,
-                        own[i] if i < R - SUBS else halo[i - R + SUBS],
-                        halo[i] if i < SUBS else own[i - SUBS],
-                    )
-                    for i in range(R)
-                ]
-            )
-        done = subcycles(groups, wide_ref)
-        for k in range(TOGETHER):
-            at = pl.multiple_of((step * TOGETHER + k) * 8, 8)
-            for i, q in enumerate(done[k]):
-                conc_ref[i, pl.ds(at, 8), :] = q
-        return carry
-
-    lax.fori_loop(0, S // 8 // TOGETHER, some_groups, 0)
-    conc = jnp.concatenate([conc_ref[i] for i in range(H)], axis=1)
-    cell = lax.broadcasted_iota(jnp.int32, (1, H * C), 1) + side * (H * C)
-    scale = jnp.where(cell < count_ref[0], DT_CHEM, 0.0).astype(F32)
-    conc = react(conc, scale, w_ref)
-    flat_ref = stage_ref.reshape(S * H, C)
-    for i in range(H):
-        for g in range(S // 8):
-            flat_ref[pl.ds(8 * g * H + i, 8, stride=H), :] = conc[8 * g : 8 * g + 8, i * C : (i + 1) * C]
-    copy = pltpu.make_async_copy(
-        stage_ref, out_hbm.at[:, pl.ds(pl.multiple_of(side * H, H), H), :], sem
-    )
-    copy.start()
-    copy.wait()
+
+def near_kernel(x_ref, winds_ref, message_ref, conc_ref, wide_ref):
+    side = is_even()
+    high = side == 1
+    edge = message_ref[pl.ds(SUBS * S, 16), :]
+    u, v = new_winds(winds_ref, edge, edge)
+    half_coefficients(u, v, high, wide_ref)
+    transport(range(S // 8), high, side, x_ref, message_ref, wide_ref, conc_ref)
+
+
+def rest_kernel(
+    scale_ref, x_ref, winds_ref, near_ref, far_ref, w_ref, near_conc_ref,
+    out_hbm, winds_out_ref, wide_ref, conc_ref, stage_ref, sems,
+):
+    side = 1 - is_even()
+    high = side == 1
+
+    def scale_of(side):
+        return scale_ref[:, pl.ds(pl.multiple_of(side * (H * C), H * C), H * C)]
+
+    def whole(ref):
+        return jnp.concatenate([ref[i] for i in range(H)], axis=1)
+
+    def put(conc, slot, side):
+        flat_ref = stage_ref.at[slot].reshape(S * H, C)
+        for i in range(H):
+            for g in range(S // 8):
+                flat_ref[pl.ds(8 * g * H + i, 8, stride=H), :] = conc[8 * g : 8 * g + 8, i * C : (i + 1) * C]
+        copy = pltpu.make_async_copy(
+            stage_ref.at[slot], out_hbm.at[:, pl.ds(pl.multiple_of(side * H, H), H), :], sems.at[slot]
+        )
+        copy.start()
+        return copy
+
+    near = near_ref[pl.ds(SUBS * S, 16), :]
+    far = far_ref[pl.ds(SUBS * S, 16), :]
+    u, v = new_winds(winds_ref, jnp.where(high, near, far), jnp.where(high, far, near))
+    winds_out_ref[0] = u[8:24]
+    winds_out_ref[1] = v[8:24]
+    half_coefficients(u, v, high, wide_ref)
+
+    conc = whole(near_conc_ref)
+    scale = scale_of(1 - side)
+    shares = [range(*b) for b in SHARES]
+    for step in range(CHEM_STEPS):
+        conc = react(conc, scale, w_ref)
+        transport(shares[step], high, side, x_ref, far_ref, wide_ref, conc_ref)
+    first = put(conc, 0, 1 - side)
+    conc = whole(conc_ref)
+    scale = scale_of(side)
+    for step in range(CHEM_STEPS):
+        conc = react(conc, scale, w_ref)
+    second = put(conc, 1, side)
+    first.wait()
+    second.wait()
+
+
+SHARES = ((0, 5), (5, 10), (10, 16))
 
 
 def on_device(tracers, winds, linear, loss, left, right, active):
@@ -227,7 +247,6 @@
     far = [(i, (i + 1 if i % 2 else i - 1) % size) for i in range(size)]
 
     vmem = pl.BlockSpec(memory_space=pltpu.VMEM)
-    smem = pl.BlockSpec(memory_space=pltpu.SMEM)
     hbm = pl.BlockSpec(memory_space=pltpu.HBM)
     params = pltpu.CompilerParams(vmem_limit_bytes=VMEM_LIMIT)
     message = jax.ShapeDtypeStruct((SUBS * S + 16, C), F32)
@@ -253,37 +272,35 @@
     )
     from_near = lax.ppermute(to_near, AXES, near)
     from_far = lax.ppermute(to_far, AXES, far)
-    w = pl.pallas_call(
+    w, scale = pl.pallas_call(
         weights_kernel,
-        out_shape=jax.ShapeDtypeStruct((OUTS, 4 * S), BF16),
-        in_specs=[vmem] * 2,
+        out_shape=[jax.ShapeDtypeStruct((OUTS, 4 * S), BF16), jax.ShapeDtypeStruct((1, R * C), F32)],
+        in_specs=[pl.BlockSpec(memory_space=pltpu.SMEM), vmem, vmem],
+        out_specs=[vmem, vmem],
+        compiler_params=params,
+    )(active, raw, loss)
+    wide = pltpu.VMEM((5, R - 2, 8, C), F32)
+    near_conc = pl.pallas_call(
+        near_kernel,
+        out_shape=jax.ShapeDtypeStruct((H, S, C), F32),
+        in_specs=[vmem] * 3,
         out_specs=vmem,
+        scratch_shapes=[wide],
         compiler_params=params,
-    )(raw, loss)
-    scratch = [
-        pltpu.VMEM((5, R - 2, 8, C), F32),
-        pltpu.VMEM((H, S, C), F32),
-        pltpu.VMEM((S, H, C), F32),
-        pltpu.SemaphoreType.DMA,
-    ]
-    whole = jax.ShapeDtypeStruct((S, R, C), F32)
-    half = pl.pallas_call(
-        functools.partial(half_kernel, False),
-        out_shape=whole,
-        in_specs=[smem] + [vmem] * 4,
-        out_specs=hbm,
-        scratch_shapes=scratch,
+    )(x, winds, from_near)
+    return pl.pallas_call(
+        rest_kernel,
+        out_shape=[jax.ShapeDtypeStruct((S, R, C), F32), jax.ShapeDtypeStruct((2, R, C), F32)],
+        in_specs=[vmem] * 7,
+        out_specs=[hbm, vmem],
+        scratch_shapes=[
+            wide,
+            pltpu.VMEM((H, S, C), F32),
+            pltpu.VMEM((2, S, H, C), F32),
+            pltpu.SemaphoreType.DMA((2,)),
+        ],
         compiler_params=params,
-    )(active, x, winds, from_near, w)
-    return pl.pallas_call(
-        functools.partial(half_kernel, True),
-        out_shape=[whole, jax.ShapeDtypeStruct((2, R, C), F32)],
-        in_specs=[smem] + [vmem] * 5 + [hbm],
-        out_specs=[hbm, vmem],
-        scratch_shapes=scratch,
-        input_output_aliases={6: 0},
-        compiler_params=params,
-    )(active, x, winds, from_far, w, from_near, half)
+    )(scale, x, winds, from_near, from_far, w, near_conc)
 
 
 def solution(mesh):

time: 29.1 us -> 27.1 us (0.931)
  Pallas kernels: 18.5 us -> 12.9 us
  waiting for transfers between devices: 0.01 us -> 3.64 us
    pallas_call x3, Pallas kernels: 17.1 us -> 11.5 us  [the longest x1 9.6 us: on_device(): pl.pallas_call(rest_kernel, out_shape=[jax.ShapeDtypeStruct((S, R, C), F3...]
    ppermute x1, waiting for transfers between devices: 0.01 us -> 3.64 us  [on_device(): from_far = lax.ppermute(to_far, AXES, far)]
  transfers between devices with their start and end apart: 2 -> 2, of which waited for: 0 -> 1; matrix products, arithmetic and copies ran while one was open for 0% -> 0% of each run, Pallas kernels for 29% -> 7%
where the time goes in v2:
time: 27.1 us; the launch traced here: 27 us
  Pallas kernels  12.9 us (48%)
  starting transfers between devices  9.07 us (33%)
  waiting for transfers between devices  3.64 us (13%)
  between operations  1.32 us (5%)
    pallas_call x1, Pallas kernels, on_device(): pl.pallas_call(rest_kernel, out_shape=[jax.ShapeDtypeStruct((S, R, C), F3...  9.6 us
    ppermute x1, starting transfers between devices, on_device(): from_far = lax.ppermute(to_far, AXES, far)  6.52 us
    ppermute x1, waiting for transfers between devices, on_device(): from_far = lax.ppermute(to_far, AXES, far)  3.64 us
    ppermute x1, starting transfers between devices, on_device(): from_near = lax.ppermute(to_near, AXES, near)  2.55 us
    pallas_call x1, Pallas kernels, on_device(): pl.pallas_call(near_kernel, out_shape=jax.ShapeDtypeStruct((H, S, C), F32...  1.71 us
    pallas_call x1, Pallas kernels, on_device(): pl.pallas_call(pack_kernel, out_shape=[message, message, jax.ShapeDtypeSt...  1.45 us
  transfers between devices with their start and end apart: 2, of which 1 were waited for; matrix products, arithmetic and copies ran while one was open for 0% of the time, Pallas kernels for 7%

profile of v2, /device:TPU:1, one launch (start us, length us, event | category | flops | bytes accessed | tf_op | source)
XLA Modules:
  0.0 27.0 jit_solution(13215395787016057552)
XLA Ops:
  0.6 1.4 %shard_map.86 = (f32[528,128]{1,0:T(8,128)S(1)}, f32[528,128]{1,0:T(8,128)S(1)}, f32[2048,128]{1,0:T(8,128)S(1)}, f32[2,16,128]{2,1,0:T(8,128)S(1)}, f32[9,128,128]{2,1,0:T(8,128)S(1)}, /*index=5*/f32[1,128]{1,0:T(1,128)S(1)}) custom-call(f32[2048,128]{1,0:T(8,128)} %bitcast.2, f32[2,16,128]{2,1,0:T(8,128)} %winds_hbm.1, f32[128,128]{1,0:T(8,128)} %linear_hbm.1, ...), custom_call_target="tpu_custom_call" | custom-call | tf_op jit(solution)/shard_map/pallas_call | solution.py:253
  2.1 2.6 %collective-permute-start = (f32[528,128]{1,0:T(8,128)S(1)}, f32[528,128]{1,0:T(8,128)S(1)}, u32[]{:S(2)}, u32[]{:S(2)}) collective-permute-start(f32[528,128]{1,0:T(8,128)S(1)} %get-tuple-element.15), channel_id=1, source_target_pairs={{0,1},{1,0},{2,3},{3,2},{4,5},{5,4},{6,7},{7,6},{8,9},{9,8},{10,11... | collective-permute-start | bytes 811016 | tf_op jit(solution)/shard_map/ppermute | solution.py:273
  4.6 6.5 %collective-permute-start.1 = (f32[528,128]{1,0:T(8,128)S(1)}, f32[528,128]{1,0:T(8,128)S(1)}, u32[]{:S(2)}, u32[]{:S(2)}) collective-permute-start(f32[528,128]{1,0:T(8,128)S(1)} %get-tuple-element.16), channel_id=1, source_target_pairs={{0,255},{1,2},{2,1},{3,4},{4,3},{5,6},{6,5},{7,8},{8,7},{9,10},{10... | collective-permute-start | bytes 811016 | tf_op jit(solution)/shard_map/ppermute | solution.py:274
  11.8 0.2 shard_map.87
  12.0 0.0 collective-permute-done.message_ref.near_ref
  12.0 1.7 %shard_map.88.near_conc_ref = f32[8,128,128]{2,1,0:T(8,128)S(1)} custom-call(f32[2048,128]{1,0:T(8,128)S(1)} %get-tuple-element.13.x_ref, f32[2,16,128]{2,1,0:T(8,128)S(1)} %get-tuple-element.14.winds_ref, f32[528,128]{1,0:T(8,128)S(1)} %collective-permute-done.message_ref.near_ref), custom_call_target="tpu_custom_call" | custom-call | tf_op jit(solution)/shard_map/pallas_call | solution.py:283
  13.7 3.6 %collective-permute-done.1.far_ref = f32[528,128]{1,0:T(8,128)S(1)} collective-permute-done((f32[528,128]{1,0:T(8,128)S(1)}, f32[528,128]{1,0:T(8,128)S(1)}, u32[]{:S(2)}, u32[]{:S(2)}) %collective-permute-start.1) | collective-permute-done | bytes 270368 | tf_op jit(solution)/shard_map/ppermute | solution.py:274
  17.4 9.6 %shard_map.89 = (f32[128,16,128]{2,1,0:T(8,128)}, f32[2,16,128]{2,1,0:T(8,128)}) custom-call(f32[1,2048]{1,0:T(1,128)S(1)} %get-tuple-element.12.scale_ref, f32[2048,128]{1,0:T(8,128)S(1)} %get-tuple-element.13.x_ref, f32[2,16,128]{2,1,0:T(8,128)S(1)} %get-tuple-element.14.winds_ref, f32[528,128]{1,0:T(8,128)S(1)} %collective-permute-done.message_ref.near_ref, ...), custom_call_target="tpu_custom_call" | custom-call | tf_op jit(solution)/shard_map/pallas_call | solution.py:291
Async XLA Ops:
  2.1 9.9 %collective-permute-start = (f32[528,128]{1,0:T(8,128)S(1)}, f32[528,128]{1,0:T(8,128)S(1)}, u32[]{:S(2)}, u32[]{:S(2)}) collective-permute-start(f32[528,128]{1,0:T(8,128)S(1)} %get-tuple-element.15), channel_id=1, source_target_pairs={{0,1},{1,0},{2,3},{3,2},{4,5},{5,4},{6,7},{7,6},{8,9},{9,8},{10,11... | collective-permute-start | bytes 811016 | tf_op jit(solution)/shard_map/ppermute | solution.py:273
  4.6 12.7 %collective-permute-start.1 = (f32[528,128]{1,0:T(8,128)S(1)}, f32[528,128]{1,0:T(8,128)S(1)}, u32[]{:S(2)}, u32[]{:S(2)}) collective-permute-start(f32[528,128]{1,0:T(8,128)S(1)} %get-tuple-element.16), channel_id=1, source_target_pairs={{0,255},{1,2},{2,1},{3,4},{4,3},{5,6},{6,5},{7,8},{8,7},{9,10},{10... | collective-permute-start | bytes 811016 | tf_op jit(solution)/shard_map/ppermute | solution.py:274

commit v3 on v2

--- a/solution.py
+++ b/solution.py
@@ -171,6 +171,14 @@
 H = R // 2
 
 
+def scale_of(scale_ref, side):
+    return scale_ref[:, pl.ds(pl.multiple_of(side * (H * C), H * C), H * C)]
+
+
+def whole(ref):
+    return jnp.concatenate([ref[i] for i in range(H)], axis=1)
+
+
 def new_winds(winds_ref, lower, upper):
     return wind_step(
         *[jnp.concatenate([lower[k * 8 : k * 8 + 8], winds_ref[k], upper[k * 8 : k * 8 + 8]], axis=0) for k in range(2)]
@@ -182,13 +190,18 @@
     coefficients(u, v, wide_ref, range(5, 5 + R - 2))
 
 
-def near_kernel(x_ref, winds_ref, message_ref, conc_ref, wide_ref):
+def near_kernel(scale_ref, x_ref, winds_ref, message_ref, w_ref, out_ref, wide_ref, conc_ref):
     side = is_even()
     high = side == 1
     edge = message_ref[pl.ds(SUBS * S, 16), :]
     u, v = new_winds(winds_ref, edge, edge)
     half_coefficients(u, v, high, wide_ref)
     transport(range(S // 8), high, side, x_ref, message_ref, wide_ref, conc_ref)
+    conc = whole(conc_ref)
+    for _ in range(NEAR_STEPS):
+        conc = react(conc, scale_of(scale_ref, side), w_ref)
+    for i in range(H):
+        out_ref[i] = conc[:, i * C : (i + 1) * C]
 
 
 def rest_kernel(
@@ -197,12 +210,6 @@
 ):
     side = 1 - is_even()
     high = side == 1
-
-    def scale_of(side):
-        return scale_ref[:, pl.ds(pl.multiple_of(side * (H * C), H * C), H * C)]
-
-    def whole(ref):
-        return jnp.concatenate([ref[i] for i in range(H)], axis=1)
 
     def put(conc, slot, side):
         flat_ref = stage_ref.at[slot].reshape(S * H, C)
@@ -223,14 +230,13 @@
     half_coefficients(u, v, high, wide_ref)
 
     conc = whole(near_conc_ref)
-    scale = scale_of(1 - side)
-    shares = [range(*b) for b in SHARES]
-    for step in range(CHEM_STEPS):
+    scale = scale_of(scale_ref, 1 - side)
+    for share in SHARES:
         conc = react(conc, scale, w_ref)
-        transport(shares[step], high, side, x_ref, far_ref, wide_ref, conc_ref)
+        transport(range(*share), high, side, x_ref, far_ref, wide_ref, conc_ref)
     first = put(conc, 0, 1 - side)
     conc = whole(conc_ref)
-    scale = scale_of(side)
+    scale = scale_of(scale_ref, side)
     for step in range(CHEM_STEPS):
         conc = react(conc, scale, w_ref)
     second = put(conc, 1, side)
@@ -238,7 +244,8 @@
     second.wait()
 
 
-SHARES = ((0, 5), (5, 10), (10, 16))
+NEAR_STEPS = 2
+SHARES = ((0, 16),)
 
 
 def on_device(tracers, winds, linear, loss, left, right, active):
@@ -283,11 +290,11 @@
     near_conc = pl.pallas_call(
         near_kernel,
         out_shape=jax.ShapeDtypeStruct((H, S, C), F32),
-        in_specs=[vmem] * 3,
+        in_specs=[vmem] * 5,
         out_specs=vmem,
-        scratch_shapes=[wide],
+        scratch_shapes=[wide, pltpu.VMEM((H, S, C), F32)],
         compiler_params=params,
-    )(x, winds, from_near)
+    )(scale, x, winds, from_near, w)
     return pl.pallas_call(
         rest_kernel,
         out_shape=[jax.ShapeDtypeStruct((S, R, C), F32), jax.ShapeDtypeStruct((2, R, C), F32)],

time: 27.1 us -> 24.6 us (0.908)
  waiting for transfers between devices: 3.64 us -> 1.34 us
    pallas_call x1, Pallas kernels: 9.6 us -> 7.15 us  [on_device(): pl.pallas_call(rest_kernel, out_shape=[jax.ShapeDtypeStruct((S, R, C), F3...]
    ppermute x1, waiting for transfers between devices: 3.64 us -> 1.34 us  [on_device(): from_far = lax.ppermute(to_far, AXES, far)]
    pallas_call x1, Pallas kernels: 1.71 us -> 4.01 us  [on_device(): pl.pallas_call(near_kernel, out_shape=jax.ShapeDtypeStruct((H, S, C), F32...]
  transfers between devices with their start and end apart: 2 -> 2, of which waited for: 1 -> 1; matrix products, arithmetic and copies ran while one was open for 0% -> 0% of each run, Pallas kernels for 7% -> 17%
where the time goes in v3:
time: 24.6 us; the launch traced here: 24.5 us
  Pallas kernels  12.8 us (52%)
  starting transfers between devices  9.07 us (37%)
  waiting for transfers between devices  1.34 us (5%)
  between operations  1.32 us (5%)
    pallas_call x1, Pallas kernels, on_device(): pl.pallas_call(rest_kernel, out_shape=[jax.ShapeDtypeStruct((S, R, C), F3...  7.15 us
    ppermute x1, starting transfers between devices, on_device(): from_far = lax.ppermute(to_far, AXES, far)  6.52 us
    pallas_call x1, Pallas kernels, on_device(): pl.pallas_call(near_kernel, out_shape=jax.ShapeDtypeStruct((H, S, C), F32...  4.01 us
    ppermute x1, starting transfers between devices, on_device(): from_near = lax.ppermute(to_near, AXES, near)  2.55 us
    pallas_call x1, Pallas kernels, on_device(): pl.pallas_call(pack_kernel, out_shape=[message, message, jax.ShapeDtypeSt...  1.45 us
    ppermute x1, waiting for transfers between devices, on_device(): from_far = lax.ppermute(to_far, AXES, far)  1.34 us
  transfers between devices with their start and end apart: 2, of which 1 were waited for; matrix products, arithmetic and copies ran while one was open for 0% of the time, Pallas kernels for 17%

profile of v3, /device:TPU:1, one launch (start us, length us, event | category | flops | bytes accessed | tf_op | source)
XLA Modules:
  0.0 24.5 jit_solution(7274205494867353644)
XLA Ops:
  0.6 1.4 %shard_map.86 = (f32[528,128]{1,0:T(8,128)S(1)}, f32[528,128]{1,0:T(8,128)S(1)}, f32[2048,128]{1,0:T(8,128)S(1)}, f32[2,16,128]{2,1,0:T(8,128)S(1)}, f32[9,128,128]{2,1,0:T(8,128)S(1)}, /*index=5*/f32[1,128]{1,0:T(1,128)S(1)}) custom-call(f32[2048,128]{1,0:T(8,128)} %bitcast.2, f32[2,16,128]{2,1,0:T(8,128)} %winds_hbm.1, f32[128,128]{1,0:T(8,128)} %linear_hbm.1, ...), custom_call_target="tpu_custom_call" | custom-call | tf_op jit(solution)/shard_map/pallas_call | solution.py:260
  2.1 2.6 %collective-permute-start = (f32[528,128]{1,0:T(8,128)S(1)}, f32[528,128]{1,0:T(8,128)S(1)}, u32[]{:S(2)}, u32[]{:S(2)}) collective-permute-start(f32[528,128]{1,0:T(8,128)S(1)} %get-tuple-element.15), channel_id=1, source_target_pairs={{0,1},{1,0},{2,3},{3,2},{4,5},{5,4},{6,7},{7,6},{8,9},{9,8},{10,11... | collective-permute-start | bytes 811016 | tf_op jit(solution)/shard_map/ppermute | solution.py:280
  4.6 6.5 %collective-permute-start.1 = (f32[528,128]{1,0:T(8,128)S(1)}, f32[528,128]{1,0:T(8,128)S(1)}, u32[]{:S(2)}, u32[]{:S(2)}) collective-permute-start(f32[528,128]{1,0:T(8,128)S(1)} %get-tuple-element.16), channel_id=1, source_target_pairs={{0,255},{1,2},{2,1},{3,4},{4,3},{5,6},{6,5},{7,8},{8,7},{9,10},{10... | collective-permute-start | bytes 811016 | tf_op jit(solution)/shard_map/ppermute | solution.py:281
  11.8 0.2 shard_map.87
  12.0 0.0 collective-permute-done.message_ref.near_ref
  12.0 4.0 %shard_map.88.near_conc_ref = f32[8,128,128]{2,1,0:T(8,128)S(1)} custom-call(f32[1,2048]{1,0:T(1,128)S(1)} %get-tuple-element.12.scale_ref, f32[2048,128]{1,0:T(8,128)S(1)} %get-tuple-element.13.x_ref, f32[2,16,128]{2,1,0:T(8,128)S(1)} %get-tuple-element.14.winds_ref, f32[528,128]{1,0:T(8,128)S(1)} %collective-permute-done.message_ref.near_ref, ...), custom_call_target="tpu_custom_call" | custom-call | tf_op jit(solution)/shard_map/pallas_call | solution.py:290
  16.0 1.3 %collective-permute-done.1.far_ref = f32[528,128]{1,0:T(8,128)S(1)} collective-permute-done((f32[528,128]{1,0:T(8,128)S(1)}, f32[528,128]{1,0:T(8,128)S(1)}, u32[]{:S(2)}, u32[]{:S(2)}) %collective-permute-start.1) | collective-permute-done | bytes 270368 | tf_op jit(solution)/shard_map/ppermute | solution.py:281
  17.4 7.1 %shard_map.89 = (f32[128,16,128]{2,1,0:T(8,128)}, f32[2,16,128]{2,1,0:T(8,128)}) custom-call(f32[1,2048]{1,0:T(1,128)S(1)} %get-tuple-element.12.scale_ref, f32[2048,128]{1,0:T(8,128)S(1)} %get-tuple-element.13.x_ref, f32[2,16,128]{2,1,0:T(8,128)S(1)} %get-tuple-element.14.winds_ref, f32[528,128]{1,0:T(8,128)S(1)} %collective-permute-done.message_ref.near_ref, ...), custom_call_target="tpu_custom_call" | custom-call | tf_op jit(solution)/shard_map/pallas_call | solution.py:298
Async XLA Ops:
  2.1 9.9 %collective-permute-start = (f32[528,128]{1,0:T(8,128)S(1)}, f32[528,128]{1,0:T(8,128)S(1)}, u32[]{:S(2)}, u32[]{:S(2)}) collective-permute-start(f32[528,128]{1,0:T(8,128)S(1)} %get-tuple-element.15), channel_id=1, source_target_pairs={{0,1},{1,0},{2,3},{3,2},{4,5},{5,4},{6,7},{7,6},{8,9},{9,8},{10,11... | collective-permute-start | bytes 811016 | tf_op jit(solution)/shard_map/ppermute | solution.py:280
  4.6 12.7 %collective-permute-start.1 = (f32[528,128]{1,0:T(8,128)S(1)}, f32[528,128]{1,0:T(8,128)S(1)}, u32[]{:S(2)}, u32[]{:S(2)}) collective-permute-start(f32[528,128]{1,0:T(8,128)S(1)} %get-tuple-element.16), channel_id=1, source_target_pairs={{0,255},{1,2},{2,1},{3,4},{4,3},{5,6},{6,5},{7,8},{8,7},{9,10},{10... | collective-permute-start | bytes 811016 | tf_op jit(solution)/shard_map/ppermute | solution.py:281

commit v4 on v2

v4 whole, which is shorter than its diff:
```python
import functools

import jax
import jax.numpy as jnp
from jax import lax
from jax.experimental import pallas as pl
from jax.experimental.pallas import tpu as pltpu
from jax.sharding import PartitionSpec as P

SUBS = 4
CHEM_STEPS = 3
PAIRS = 4
DT_WIND = 0.1
VISCOSITY = 0.2
DT_TRACER = 0.1
DT_CHEM = 0.1

AXES = ("tile", "trac")
RUN = 8
S = 128
R = 16
C = 128
OUTS = S * (1 + 2 * PAIRS)
F32 = jnp.float32
BF16 = jnp.bfloat16
VMEM_LIMIT = 48 * 1024 * 1024


def lanes(x, shift):
    return pltpu.roll(x, shift % C, 1)


def rows_rolled(x, shift):
    return pltpu.roll(x, shift % x.shape[0], 0)


def is_even():
    return 1 - lax.axis_index(AXES) % 2


def far_part(far_refs, at, size):
    late = lax.axis_index(AXES) % RUN == RUN - 1
    return jnp.where(late, far_refs[1][pl.ds(at, size), :], far_refs[0][pl.ds(at, size), :])


def pack_kernel(
    x_hbm, winds_hbm, linear_hbm, loss_hbm, left_hbm, right_hbm,
    near_ref, far_ref, x_ref, winds_ref, raw_ref, loss_ref, sems,
):
    even = is_even()
    moves = []
    for k in range(CHUNKS):
        part = pl.ds(k * (S * R // CHUNKS), S * R // CHUNKS)
        moves.append((x_hbm.at[part], x_ref.at[part]))
    moves.append((winds_hbm, winds_ref))
    moves.append((left_hbm, raw_ref.at[pl.ds(1, PAIRS)]))
    moves.append((right_hbm, raw_ref.at[pl.ds(1 + PAIRS, PAIRS)]))
    moves.append((linear_hbm, raw_ref.at[0]))
    moves.append((loss_hbm, loss_ref))
    copies = [pltpu.make_async_copy(a, b, sems.at[i]) for i, (a, b) in enumerate(moves)]
    for copy in copies:
        copy.start()
    for k in range(CHUNKS):
        copies[k].wait()
        for ref, side in ((near_ref, even), (far_ref, 1 - even)):
            for r in range(SUBS):
                for g in range(k * S // 8 // CHUNKS, (k + 1) * S // 8 // CHUNKS):
                    at = 8 * g * R + r + side * (R - SUBS)
                    ref[pl.ds(r * S + 8 * g, 8), :] = x_ref[pl.ds(at, 8, stride=R), :]
    copies[CHUNKS].wait()
    for ref, side in ((near_ref, even), (far_ref, 1 - even)):
        for k in range(2):
            ref[pl.ds(SUBS * S + 8 * k, 8), :] = winds_ref[k, pl.ds(pl.multiple_of(side * 8, 8), 8), :]
    for copy in copies[CHUNKS + 1 :]:
        copy.wait()


def weights_kernel(raw_ref, loss_ref, w_ref):
    row = lax.broadcasted_iota(jnp.int32, (S, S), 0)
    col = lax.broadcasted_iota(jnp.int32, (S, S), 1)
    diagonal = jnp.where(row == col, jnp.broadcast_to(loss_ref[...], (S, S)), 0.0)
    parts = [raw_ref[0] - diagonal]
    for p in range(PAIRS):
        parts += [raw_ref[1 + p], raw_ref[1 + PAIRS + p]]
    for i, part in enumerate(parts):
        hi = part.astype(BF16)
        lo = (part - hi.astype(F32)).astype(BF16)
        w_ref[pl.ds(i * S, S), pl.ds(0, S)] = hi
        w_ref[pl.ds(i * S, S), pl.ds(S, S)] = hi
        w_ref[pl.ds(i * S, S), pl.ds(2 * S, S)] = lo
        w_ref[pl.ds(i * S, S), pl.ds(3 * S, S)] = lo


def tendency(u, v):
    out = []
    for f in (u, v):
        east, west, north, south = lanes(f, -1), lanes(f, 1), rows_rolled(f, -1), rows_rolled(f, 1)
        along = (east - west) * 0.5
        across = (north - south) * 0.5
        spread = east + west + north + south - 4.0 * f
        out.append(-(u * along + v * across) + VISCOSITY * spread)
    return out


def wind_step(u, v):
    du, dv = tendency(u, v)
    fu, fv = u + DT_WIND * du, v + DT_WIND * dv
    du, dv = tendency(fu, fv)
    su = 0.75 * u + 0.25 * (fu + DT_WIND * du)
    sv = 0.75 * v + 0.25 * (fv + DT_WIND * dv)
    du, dv = tendency(su, sv)
    return (
        u / 3.0 + 2.0 / 3.0 * (su + DT_WIND * du),
        v / 3.0 + 2.0 / 3.0 * (sv + DT_WIND * dv),
    )


def row_of(m):
    return is_even() * (R - 1 - 2 * m) + m


def near_row(m):
    return is_even() * (-1 - m) + (1 - is_even()) * (m + SUBS)


def far_row(m):
    return is_even() * (R + SUBS - 1 - m) + (1 - is_even()) * (m - R)


def coefficients(u, v, coef_ref, wide_ref, ms):
    north = -DT_TRACER * rows_rolled(jnp.minimum(v, 0.0), -1)
    south = DT_TRACER * rows_rolled(jnp.maximum(v, 0.0), 1)
    even = is_even() == 1
    coef_ref[0] = 1.0 - DT_TRACER * (jnp.abs(u) + jnp.abs(v))
    coef_ref[1] = -DT_TRACER * lanes(jnp.minimum(u, 0.0), -1)
    coef_ref[2] = DT_TRACER * lanes(jnp.maximum(u, 0.0), 1)
    coef_ref[3] = jnp.where(even, south, north)
    coef_ref[4] = jnp.where(even, north, south)
    for i, m in enumerate(ms):
        for k in range(5):
            wide_ref[k, i] = jnp.broadcast_to(coef_ref[k, pl.ds(row_of(m) + 8, 1), :], (8, C))


def subcycle(states, ms, wide_ref, first):
    done = {}
    for m in ms:
        k = [wide_ref[j, m - first] for j in range(5)]
        done[m] = [
            k[0] * q + k[1] * lanes(q, -1) + k[2] * lanes(q, 1) + (k[3] * above + k[4] * below)
            for q, above, below in zip(states[m], states[m + 1], states[m - 1])
        ]
    return done


def own_rows(x_ref, ms):
    return {m: [x_ref[pl.ds(8 * g * R + row_of(m), 8, stride=R), :] for g in range(S // 8)] for m in ms}


def stored(ref, slot):
    return [ref[slot, pl.ds(8 * g, 8), :] for g in range(S // 8)]


def store(ref, slot, groups):
    for g, q in enumerate(groups):
        ref[slot, pl.ds(8 * g, 8), :] = q


def halo_rows(part, ms, place):
    return {m: [part(pl.multiple_of(place(m) * S + 8 * g, 8), 8) for g in range(S // 8)] for m in ms}


def react(conc, scale, w_ref):
    hi = conc.astype(BF16)
    lo = (conc - hi.astype(F32)).astype(BF16)
    both = jnp.concatenate([hi, lo, hi, lo], axis=0)
    y = jnp.dot(w_ref[...], both, preferred_element_type=F32)
    rate = y[0:S]
    for p in range(PAIRS):
        at = (1 + 2 * p) * S
        rate = rate + y[at : at + S] * y[at + S : at + 2 * S]
    return conc + rate * scale


CHUNKS = 4
H = R // 2


def scale_of(count_ref, ms):
    col = lax.broadcasted_iota(jnp.int32, (1, C), 1)
    return jnp.concatenate(
        [jnp.where(col + row_of(m) * C < count_ref[0], DT_CHEM, 0.0).astype(F32) for m in ms], axis=1
    )


def whole(ref, slots):
    return jnp.concatenate([ref[i] for i in slots], axis=1)


def new_winds(winds_ref, near_part, far_part):
    even = is_even() == 1
    field = []
    for k in range(2):
        near = near_part(SUBS * S + 8 * k, 8)
        far = far_part(SUBS * S + 8 * k, 8)
        field.append(
            jnp.concatenate([jnp.where(even, far, near), winds_ref[k], jnp.where(even, near, far)], axis=0)
        )
    return wind_step(*field)


def part_of(ref, at, size):
    return ref[pl.ds(at, size), :]


FAR_FIRST = R - SUBS
SAVED = 2 * (SUBS - 1) + 1


def near_kernel(count_ref, x_ref, winds_ref, near_ref, w_ref, conc_ref, saved_ref, coef_ref, wide_ref):
    near = functools.partial(part_of, near_ref)
    u, v = new_winds(winds_ref, near, near)
    coefficients(u, v, coef_ref, wide_ref, range(1 - SUBS, FAR_FIRST))
    states = own_rows(x_ref, range(FAR_FIRST + 1)) | halo_rows(near, range(-SUBS, 0), near_row)
    for sub in range(SUBS):
        states = subcycle(states, range(1 - SUBS + sub, FAR_FIRST - sub), wide_ref, 1 - SUBS)
        last = FAR_FIRST - sub - 1
        if sub < SUBS - 1:
            store(saved_ref, 2 * sub, states[last - 1])
            store(saved_ref, 2 * sub + 1, states[last])
        else:
            store(saved_ref, 2 * sub, states[last])
    for m in range(H):
        store(conc_ref, m, states[m])
    conc = whole(conc_ref, range(H))
    for _ in range(NEAR_STEPS):
        conc = react(conc, scale_of(count_ref, range(H)), w_ref)
    for m in range(H):
        conc_ref[m] = conc[:, m * C : (m + 1) * C]


def far_transport(x_ref, far, saved_ref, wide_ref, conc_ref):
    states = own_rows(x_ref, range(FAR_FIRST - 1, R)) | halo_rows(far, range(R, R + SUBS), far_row)
    for sub in range(SUBS):
        first = FAR_FIRST - sub
        states = subcycle(states, range(first, first + H - 1), wide_ref, FAR_FIRST - SUBS + 1)
        if sub < SUBS - 1:
            states[first - 2] = stored(saved_ref, 2 * sub)
            states[first - 1] = stored(saved_ref, 2 * sub + 1)
    store(conc_ref, 0, stored(saved_ref, SAVED - 1))
    for m in range(H + 1, R):
        store(conc_ref, m - H, states[m])


def rest_kernel(
    count_ref, x_ref, winds_ref, near_ref, late_ref, far_ref, w_ref, near_conc_ref, saved_ref,
    out_hbm, winds_out_ref, coef_ref, wide_ref, conc_ref, stage_ref, sems,
):
    def put(conc, slot, high):
        flat_ref = stage_ref.at[slot].reshape(S * H, C)
        for i in range(H):
            at = is_even() * (H - 1 - 2 * i) + i
            for g in range(S // 8):
                flat_ref[pl.ds(8 * g * H + at, 8, stride=H), :] = conc[8 * g : 8 * g + 8, i * C : (i + 1) * C]
        copy = pltpu.make_async_copy(
            stage_ref.at[slot], out_hbm.at[:, pl.ds(pl.multiple_of(high * H, H), H), :], sems.at[slot]
        )
        copy.start()
        return copy

    far = functools.partial(far_part, (far_ref, late_ref))
    u, v = new_winds(winds_ref, functools.partial(part_of, near_ref), far)
    winds_out_ref[0] = u[8:24]
    winds_out_ref[1] = v[8:24]
    coefficients(u, v, coef_ref, wide_ref, range(FAR_FIRST - SUBS + 1, R + SUBS - 1))
    conc = whole(near_conc_ref, range(H))
    for step in range(NEAR_STEPS, CHEM_STEPS):
        conc = react(conc, scale_of(count_ref, range(H)), w_ref)
    first = put(conc, 0, is_even())
    far_transport(x_ref, far, saved_ref, wide_ref, conc_ref)
    conc = whole(conc_ref, range(H))
    for step in range(CHEM_STEPS):
        conc = react(conc, scale_of(count_ref, range(H, R)), w_ref)
    second = put(conc, 1, 1 - is_even())
    first.wait()
    second.wait()


NEAR_STEPS = 2


def on_device(tracers, winds, linear, loss, left, right, active):
    size = lax.axis_size(AXES)
    near = [(i, i ^ 1) for i in range(size)]
    up = [(i, (i + 1) % size) for i in range(1, size, 2)]
    late = [(b, a) for a, b in up if a % RUN == RUN - 1]
    far = up + [(b, a) for a, b in up if a % RUN != RUN - 1]
    smem = pl.BlockSpec(memory_space=pltpu.SMEM)
    vmem = pl.BlockSpec(memory_space=pltpu.VMEM)
    hbm = pl.BlockSpec(memory_space=pltpu.HBM)
    params = pltpu.CompilerParams(vmem_limit_bytes=VMEM_LIMIT)
    message = jax.ShapeDtypeStruct((SUBS * S + 16, C), F32)
    to_near, to_far, x, winds, raw, loss = pl.pallas_call(
        pack_kernel,
        out_shape=[
            message,
            message,
            jax.ShapeDtypeStruct((S * R, C), F32),
            jax.ShapeDtypeStruct((2, R, C), F32),
            jax.ShapeDtypeStruct((1 + 2 * PAIRS, S, S), F32),
            jax.ShapeDtypeStruct((1, S), F32),
        ],
        in_specs=[hbm] * 6,
        out_specs=[vmem] * 6,
        scratch_shapes=[pltpu.SemaphoreType.DMA((CHUNKS + 5,))],
        compiler_params=params,
    )(
        *[
            pltpu.with_memory_space_constraint(a, pltpu.HBM)
            for a in (tracers.reshape(S * R, C), winds, linear, loss.reshape(1, S), left, right)
        ]
    )
    from_near = lax.ppermute(to_near, AXES, near)
    from_far = lax.ppermute(to_far, AXES, far)
    from_late = lax.ppermute(to_far, AXES, late)
    w = pl.pallas_call(
        weights_kernel,
        out_shape=jax.ShapeDtypeStruct((OUTS, 4 * S), BF16),
        in_specs=[vmem] * 2,
        out_specs=vmem,
        compiler_params=params,
    )(raw, loss)
    coef = pltpu.VMEM((5, R + 16, C), F32)
    half = jax.ShapeDtypeStruct((H, S, C), F32)
    conc, saved = pl.pallas_call(
        near_kernel,
        out_shape=[half, jax.ShapeDtypeStruct((SAVED, S, C), F32)],
        in_specs=[smem] + [vmem] * 4,
        out_specs=[vmem] * 2,
        scratch_shapes=[coef, pltpu.VMEM((5, FAR_FIRST + SUBS - 1, 8, C), F32)],
        compiler_params=params,
    )(active, x, winds, from_near, w)
    return pl.pallas_call(
        rest_kernel,
        out_shape=[jax.ShapeDtypeStruct((S, R, C), F32), jax.ShapeDtypeStruct((2, R, C), F32)],
        in_specs=[smem] + [vmem] * 8,
        out_specs=[hbm, vmem],
        scratch_shapes=[
            coef,
            pltpu.VMEM((5, H + SUBS - 2, 8, C), F32),
            pltpu.VMEM((H, S, C), F32),
            pltpu.VMEM((2, S, H, C), F32),
            pltpu.SemaphoreType.DMA((2,)),
        ],
        compiler_params=params,
    )(active, x, winds, from_near, from_late, from_far, w, conc, saved)


def solution(mesh):
    grid = P(None, ("tile", "trac"), None)
    return jax.shard_map(
        on_device,
        mesh=mesh,
        in_specs=(grid, grid, P(), P(), P(), P(), P(("tile", "trac"))),
        out_specs=(grid, grid),
        check_vma=False,
    )
```

time: 27.1 us -> 26.7 us (0.985)
  waiting for transfers between devices: 3.64 us -> 0.01 us
  starting transfers between devices: 9.07 us -> 12.3 us
    ppermute x0 -> x1, starting transfers between devices: none -> 8.45 us  [on_device(): from_late = lax.ppermute(to_far, AXES, late)]
    ppermute x1, starting transfers between devices: 6.52 us -> 1.28 us  [on_device(): from_far = lax.ppermute(to_far, AXES, far)]
    ppermute x1, waiting for transfers between devices: 3.64 us -> 0.01 us  [on_device(): from_far = lax.ppermute(to_far, AXES, far)]
    pallas_call x1, Pallas kernels: 9.6 us -> 6.93 us  [on_device(): pl.pallas_call(rest_kernel, out_shape=[jax.ShapeDtypeStruct((S, R, C), F3...]
    pallas_call x2, Pallas kernels: 1.88 us -> 4.37 us  [the longest x1 4.21 us: on_device(): pl.pallas_call(near_kernel, out_shape=[half, jax.ShapeDtypeStruct((SAVED,...]
  transfers between devices with their start and end apart: 2 -> 3, of which waited for: 1 -> 0; matrix products, arithmetic and copies ran while one was open for 0% -> 0% of each run, Pallas kernels for 7% -> 17%
where the time goes in v4:
time: 26.7 us; the launch traced here: 26.4 us
  Pallas kernels  12.7 us (48%)
  starting transfers between devices  12.3 us (46%)
  between operations  1.34 us (5%)
    ppermute x1, starting transfers between devices, on_device(): from_late = lax.ppermute(to_far, AXES, late)  8.45 us
    pallas_call x1, Pallas kernels, on_device(): pl.pallas_call(rest_kernel, out_shape=[jax.ShapeDtypeStruct((S, R, C), F3...  6.93 us
    pallas_call x1, Pallas kernels, on_device(): pl.pallas_call(near_kernel, out_shape=[half, jax.ShapeDtypeStruct((SAVED,...  4.21 us
    ppermute x1, starting transfers between devices, on_device(): from_near = lax.ppermute(to_near, AXES, near)  2.55 us
    pallas_call x1, Pallas kernels, on_device(): pl.pallas_call(pack_kernel, out_shape=[message, message, jax.ShapeDtypeSt...  1.45 us
    ppermute x1, starting transfers between devices, on_device(): from_far = lax.ppermute(to_far, AXES, far)  1.28 us
  transfers between devices with their start and end apart: 3, of which 0 were waited for; matrix products, arithmetic and copies ran while one was open for 0% of the time, Pallas kernels for 17%

profile of v4, /device:TPU:1, one launch (start us, length us, event | category | flops | bytes accessed | tf_op | source)
XLA Modules:
  0.0 26.4 jit_solution(492945444057328258)
XLA Ops:
  0.6 1.4 %shard_map.86 = (f32[528,128]{1,0:T(8,128)S(1)}, f32[528,128]{1,0:T(8,128)S(1)}, f32[2048,128]{1,0:T(8,128)S(1)}, f32[2,16,128]{2,1,0:T(8,128)S(1)}, f32[9,128,128]{2,1,0:T(8,128)S(1)}, /*index=5*/f32[1,128]{1,0:T(1,128)S(1)}) custom-call(f32[2048,128]{1,0:T(8,128)} %bitcast.2, f32[2,16,128]{2,1,0:T(8,128)} %winds_hbm.1, f32[128,128]{1,0:T(8,128)} %linear_hbm.1, ...), custom_call_target="tpu_custom_call" | custom-call | tf_op jit(solution)/shard_map/pallas_call | solution.py:302
  2.1 2.6 %collective-permute-start = (f32[528,128]{1,0:T(8,128)S(1)}, f32[528,128]{1,0:T(8,128)S(1)}, u32[]{:S(2)}, u32[]{:S(2)}) collective-permute-start(f32[528,128]{1,0:T(8,128)S(1)} %get-tuple-element.12), channel_id=1, source_target_pairs={{0,1},{1,0},{2,3},{3,2},{4,5},{5,4},{6,7},{7,6},{8,9},{9,8},{10,11... | collective-permute-start | bytes 811016 | tf_op jit(solution)/shard_map/ppermute | solution.py:322
  4.6 1.3 %collective-permute-start.2 = (f32[528,128]{1,0:T(8,128)S(1)}, f32[528,128]{1,0:T(8,128)S(1)}, u32[]{:S(2)}, u32[]{:S(2)}) collective-permute-start(f32[528,128]{1,0:T(8,128)S(1)} %get-tuple-element.13), channel_id=1, source_target_pairs={{1,2},{3,4},{5,6},{7,8},{9,10},{11,12},{13,14},{15,16},{17,18},{19... | collective-permute-start | bytes 811016 | tf_op jit(solution)/shard_map/ppermute | solution.py:323
  5.9 8.5 %collective-permute-start.1 = (f32[528,128]{1,0:T(8,128)S(1)}, f32[528,128]{1,0:T(8,128)S(1)}, u32[]{:S(2)}, u32[]{:S(2)}) collective-permute-start(f32[528,128]{1,0:T(8,128)S(1)} %get-tuple-element.13), channel_id=1, source_target_pairs={{8,7},{16,15},{24,23},{32,31},{40,39},{48,47},{56,55},{64,63},{72,... | collective-permute-start | bytes 811016 | tf_op jit(solution)/shard_map/ppermute | solution.py:324
  15.0 0.2 shard_map.87.w_ref
  15.2 0.0 collective-permute-done.near_ref
  15.2 4.2 %shard_map.88 = (f32[8,128,128]{2,1,0:T(8,128)S(1)}, f32[7,128,128]{2,1,0:T(8,128)S(1)}) custom-call(s32[1]{0:T(128)S(6)} %copy.9.count_ref, f32[2048,128]{1,0:T(8,128)S(1)} %get-tuple-element.10.x_ref, f32[2,16,128]{2,1,0:T(8,128)S(1)} %get-tuple-element.11.winds_ref, f32[528,128]{1,0:T(8,128)S(1)} %collective-permute-done.near_ref, ...), custom_call_target="tpu_custom_call" | custom-call | tf_op jit(solution)/shard_map/pallas_call | solution.py:334
  19.4 0.0 collective-permute-done.2.far_ref
  19.4 0.0 collective-permute-done.1.late_ref
  19.5 6.9 %shard_map.89 = (f32[128,16,128]{2,1,0:T(8,128)}, f32[2,16,128]{2,1,0:T(8,128)}) custom-call(s32[1]{0:T(128)S(6)} %copy.9.count_ref, f32[2048,128]{1,0:T(8,128)S(1)} %get-tuple-element.10.x_ref, f32[2,16,128]{2,1,0:T(8,128)S(1)} %get-tuple-element.11.winds_ref, f32[528,128]{1,0:T(8,128)S(1)} %collective-permute-done.near_ref, ...), custom_call_target="tpu_custom_call" | custom-call | tf_op jit(solution)/shard_map/pallas_call | solution.py:342
Async XLA Ops:
  2.1 13.1 %collective-permute-start = (f32[528,128]{1,0:T(8,128)S(1)}, f32[528,128]{1,0:T(8,128)S(1)}, u32[]{:S(2)}, u32[]{:S(2)}) collective-permute-start(f32[528,128]{1,0:T(8,128)S(1)} %get-tuple-element.12), channel_id=1, source_target_pairs={{0,1},{1,0},{2,3},{3,2},{4,5},{5,4},{6,7},{7,6},{8,9},{9,8},{10,11... | collective-permute-start | bytes 811016 | tf_op jit(solution)/shard_map/ppermute | solution.py:322
  4.6 14.8 %collective-permute-start.2 = (f32[528,128]{1,0:T(8,128)S(1)}, f32[528,128]{1,0:T(8,128)S(1)}, u32[]{:S(2)}, u32[]{:S(2)}) collective-permute-start(f32[528,128]{1,0:T(8,128)S(1)} %get-tuple-element.13), channel_id=1, source_target_pairs={{1,2},{3,4},{5,6},{7,8},{9,10},{11,12},{13,14},{15,16},{17,18},{19... | collective-permute-start | bytes 811016 | tf_op jit(solution)/shard_map/ppermute | solution.py:323
  5.9 13.5 %collective-permute-start.1 = (f32[528,128]{1,0:T(8,128)S(1)}, f32[528,128]{1,0:T(8,128)S(1)}, u32[]{:S(2)}, u32[]{:S(2)}) collective-permute-start(f32[528,128]{1,0:T(8,128)S(1)} %get-tuple-element.13), channel_id=1, source_target_pairs={{8,7},{16,15},{24,23},{32,31},{40,39},{48,47},{56,55},{64,63},{72,... | collective-permute-start | bytes 811016 | tf_op jit(solution)/shard_map/ppermute | solution.py:324

commit v5 on v4

--- a/solution.py
+++ b/solution.py
@@ -1,5 +1,3 @@
-import functools
-
 import jax
 import jax.numpy as jnp
 from jax import lax
@@ -16,7 +14,6 @@
 DT_CHEM = 0.1
 
 AXES = ("tile", "trac")
-RUN = 8
 S = 128
 R = 16
 C = 128
@@ -36,11 +33,6 @@
 
 def is_even():
     return 1 - lax.axis_index(AXES) % 2
-
-
-def far_part(far_refs, at, size):
-    late = lax.axis_index(AXES) % RUN == RUN - 1
-    return jnp.where(late, far_refs[1][pl.ds(at, size), :], far_refs[0][pl.ds(at, size), :])
 
 
 def pack_kernel(
@@ -75,7 +67,9 @@
         copy.wait()
 
 
-def weights_kernel(raw_ref, loss_ref, w_ref):
+def weights_kernel(count_ref, raw_ref, loss_ref, w_ref, scale_ref):
+    cell = lax.broadcasted_iota(jnp.int32, (R, C), 0) * C + lax.broadcasted_iota(jnp.int32, (R, C), 1)
+    scale_ref[...] = jnp.where(cell < count_ref[0], DT_CHEM, 0.0).astype(F32)
     row = lax.broadcasted_iota(jnp.int32, (S, S), 0)
     col = lax.broadcasted_iota(jnp.int32, (S, S), 1)
     diagonal = jnp.where(row == col, jnp.broadcast_to(loss_ref[...], (S, S)), 0.0)
@@ -85,10 +79,10 @@
     for i, part in enumerate(parts):
         hi = part.astype(BF16)
         lo = (part - hi.astype(F32)).astype(BF16)
-        w_ref[pl.ds(i * S, S), pl.ds(0, S)] = hi
-        w_ref[pl.ds(i * S, S), pl.ds(S, S)] = hi
-        w_ref[pl.ds(i * S, S), pl.ds(2 * S, S)] = lo
-        w_ref[pl.ds(i * S, S), pl.ds(3 * S, S)] = lo
+        for c in range(S // B):
+            rows = pl.ds((c * len(parts) + i) * B, B)
+            for k, piece in enumerate((hi, hi, lo, lo)):
+                w_ref[rows, pl.ds(k * S, S)] = piece[c * B : (c + 1) * B]
 
 
 def tendency(u, v):
@@ -165,62 +159,68 @@
         ref[slot, pl.ds(8 * g, 8), :] = q
 
 
-def halo_rows(part, ms, place):
-    return {m: [part(pl.multiple_of(place(m) * S + 8 * g, 8), 8) for g in range(S // 8)] for m in ms}
-
-
-def react(conc, scale, w_ref):
+def halo_rows(message_ref, ms, place):
+    return {
+        m: [message_ref[pl.ds(pl.multiple_of(place(m) * S + 8 * g, 8), 8), :] for g in range(S // 8)] for m in ms
+    }
+
+
+def react_blocks(conc, scale, w_ref, apart):
     hi = conc.astype(BF16)
     lo = (conc - hi.astype(F32)).astype(BF16)
     both = jnp.concatenate([hi, lo, hi, lo], axis=0)
-    y = jnp.dot(w_ref[...], both, preferred_element_type=F32)
-    rate = y[0:S]
-    for p in range(PAIRS):
-        at = (1 + 2 * p) * S
-        rate = rate + y[at : at + S] * y[at + S : at + 2 * S]
-    return conc + rate * scale
-
-
+    size = B * (1 + 2 * PAIRS)
+    if not apart:
+        whole_y = jnp.dot(w_ref[...], both, preferred_element_type=F32)
+    for c in range(S // B):
+        if apart:
+            y = jnp.dot(w_ref[pl.ds(c * size, size), :], both, preferred_element_type=F32)
+        else:
+            y = whole_y[c * size : (c + 1) * size]
+        rate = y[0:B]
+        for p in range(PAIRS):
+            at = (1 + 2 * p) * B
+            rate = rate + y[at : at + B] * y[at + B : at + 2 * B]
+        yield conc[c * B : (c + 1) * B] + rate * scale
+
+
+def react(conc, scale, w_ref):
+    return jnp.concatenate(list(react_blocks(conc, scale, w_ref, False)), axis=0)
+
+
+B = 64
 CHUNKS = 4
 H = R // 2
 
 
-def scale_of(count_ref, ms):
-    col = lax.broadcasted_iota(jnp.int32, (1, C), 1)
-    return jnp.concatenate(
-        [jnp.where(col + row_of(m) * C < count_ref[0], DT_CHEM, 0.0).astype(F32) for m in ms], axis=1
-    )
+def scale_of(scale_ref, ms):
+    return jnp.concatenate([scale_ref[pl.ds(row_of(m), 1), :] for m in ms], axis=1)
 
 
 def whole(ref, slots):
     return jnp.concatenate([ref[i] for i in slots], axis=1)
 
 
-def new_winds(winds_ref, near_part, far_part):
+def new_winds(winds_ref, near_ref, far_ref):
     even = is_even() == 1
     field = []
     for k in range(2):
-        near = near_part(SUBS * S + 8 * k, 8)
-        far = far_part(SUBS * S + 8 * k, 8)
+        near = near_ref[pl.ds(SUBS * S + 8 * k, 8), :]
+        far = far_ref[pl.ds(SUBS * S + 8 * k, 8), :]
         field.append(
             jnp.concatenate([jnp.where(even, far, near), winds_ref[k], jnp.where(even, near, far)], axis=0)
         )
     return wind_step(*field)
 
 
-def part_of(ref, at, size):
-    return ref[pl.ds(at, size), :]
-
-
 FAR_FIRST = R - SUBS
 SAVED = 2 * (SUBS - 1) + 1
 
 
-def near_kernel(count_ref, x_ref, winds_ref, near_ref, w_ref, conc_ref, saved_ref, coef_ref, wide_ref):
-    near = functools.partial(part_of, near_ref)
-    u, v = new_winds(winds_ref, near, near)
+def near_kernel(scale_ref, x_ref, winds_ref, near_ref, w_ref, conc_ref, saved_ref, coef_ref, wide_ref):
+    u, v = new_winds(winds_ref, near_ref, near_ref)
     coefficients(u, v, coef_ref, wide_ref, range(1 - SUBS, FAR_FIRST))
-    states = own_rows(x_ref, range(FAR_FIRST + 1)) | halo_rows(near, range(-SUBS, 0), near_row)
+    states = own_rows(x_ref, range(FAR_FIRST + 1)) | halo_rows(near_ref, range(-SUBS, 0), near_row)
     for sub in range(SUBS):
         states = subcycle(states, range(1 - SUBS + sub, FAR_FIRST - sub), wide_ref, 1 - SUBS)
         last = FAR_FIRST - sub - 1
@@ -233,13 +233,13 @@
         store(conc_ref, m, states[m])
     conc = whole(conc_ref, range(H))
     for _ in range(NEAR_STEPS):
-        conc = react(conc, scale_of(count_ref, range(H)), w_ref)
+        conc = react(conc, scale_of(scale_ref, range(H)), w_ref)
     for m in range(H):
         conc_ref[m] = conc[:, m * C : (m + 1) * C]
 
 
-def far_transport(x_ref, far, saved_ref, wide_ref, conc_ref):
-    states = own_rows(x_ref, range(FAR_FIRST - 1, R)) | halo_rows(far, range(R, R + SUBS), far_row)
+def far_transport(x_ref, far_ref, saved_ref, wide_ref, conc_ref):
+    states = own_rows(x_ref, range(FAR_FIRST - 1, R)) | halo_rows(far_ref, range(R, R + SUBS), far_row)
     for sub in range(SUBS):
         first = FAR_FIRST - sub
         states = subcycle(states, range(first, first + H - 1), wide_ref, FAR_FIRST - SUBS + 1)
@@ -252,49 +252,50 @@
 
 
 def rest_kernel(
-    count_ref, x_ref, winds_ref, near_ref, late_ref, far_ref, w_ref, near_conc_ref, saved_ref,
+    scale_ref, x_ref, winds_ref, near_ref, far_ref, w_ref, near_conc_ref, saved_ref,
     out_hbm, winds_out_ref, coef_ref, wide_ref, conc_ref, stage_ref, sems,
 ):
-    def put(conc, slot, high):
+    copies = []
+
+    def put(blocks, slot, high):
         flat_ref = stage_ref.at[slot].reshape(S * H, C)
-        for i in range(H):
-            at = is_even() * (H - 1 - 2 * i) + i
-            for g in range(S // 8):
-                flat_ref[pl.ds(8 * g * H + at, 8, stride=H), :] = conc[8 * g : 8 * g + 8, i * C : (i + 1) * C]
-        copy = pltpu.make_async_copy(
-            stage_ref.at[slot], out_hbm.at[:, pl.ds(pl.multiple_of(high * H, H), H), :], sems.at[slot]
-        )
-        copy.start()
-        return copy
-
-    far = functools.partial(far_part, (far_ref, late_ref))
-    u, v = new_winds(winds_ref, functools.partial(part_of, near_ref), far)
+        for c, block in enumerate(blocks):
+            for i in range(H):
+                at = is_even() * (H - 1 - 2 * i) + i
+                for g in range(c * B // 8, (c + 1) * B // 8):
+                    row = 8 * g - c * B
+                    flat_ref[pl.ds(8 * g * H + at, 8, stride=H), :] = block[row : row + 8, i * C : (i + 1) * C]
+            part = pl.ds(c * B, B)
+            rows = pl.ds(pl.multiple_of(high * H, H), H)
+            copies.append(pltpu.make_async_copy(stage_ref.at[slot, part], out_hbm.at[part, rows, :], sems.at[slot, c]))
+            copies[-1].start()
+
+    u, v = new_winds(winds_ref, near_ref, far_ref)
     winds_out_ref[0] = u[8:24]
     winds_out_ref[1] = v[8:24]
     coefficients(u, v, coef_ref, wide_ref, range(FAR_FIRST - SUBS + 1, R + SUBS - 1))
     conc = whole(near_conc_ref, range(H))
     for step in range(NEAR_STEPS, CHEM_STEPS):
-        conc = react(conc, scale_of(count_ref, range(H)), w_ref)
-    first = put(conc, 0, is_even())
-    far_transport(x_ref, far, saved_ref, wide_ref, conc_ref)
+        conc = react(conc, scale_of(scale_ref, range(H)), w_ref)
+    put([conc[c * B : (c + 1) * B] for c in range(S // B)], 0, is_even())
+    far_transport(x_ref, far_ref, saved_ref, wide_ref, conc_ref)
     conc = whole(conc_ref, range(H))
-    for step in range(CHEM_STEPS):
-        conc = react(conc, scale_of(count_ref, range(H, R)), w_ref)
-    second = put(conc, 1, 1 - is_even())
-    first.wait()
-    second.wait()
-
-
-NEAR_STEPS = 2
+    scale = scale_of(scale_ref, range(H, R))
+    for step in range(CHEM_STEPS - 1):
+        conc = react(conc, scale, w_ref)
+    put(react_blocks(conc, scale, w_ref, True), 1, 1 - is_even())
+    for copy in copies:
+        copy.wait()
+
+
+NEAR_STEPS = 3
 
 
 def on_device(tracers, winds, linear, loss, left, right, active):
     size = lax.axis_size(AXES)
     near = [(i, i ^ 1) for i in range(size)]
-    up = [(i, (i + 1) % size) for i in range(1, size, 2)]
-    late = [(b, a) for a, b in up if a % RUN == RUN - 1]
-    far = up + [(b, a) for a, b in up if a % RUN != RUN - 1]
-    smem = pl.BlockSpec(memory_space=pltpu.SMEM)
+    far = [(i, (i + 1 if i % 2 else i - 1) % size) for i in range(size)]
+
     vmem = pl.BlockSpec(memory_space=pltpu.VMEM)
     hbm = pl.BlockSpec(memory_space=pltpu.HBM)
     params = pltpu.CompilerParams(vmem_limit_bytes=VMEM_LIMIT)
@@ -321,38 +322,37 @@
     )
     from_near = lax.ppermute(to_near, AXES, near)
     from_far = lax.ppermute(to_far, AXES, far)
-    from_late = lax.ppermute(to_far, AXES, late)
-    w = pl.pallas_call(
+    w, scale = pl.pallas_call(
         weights_kernel,
-        out_shape=jax.ShapeDtypeStruct((OUTS, 4 * S), BF16),
-        in_specs=[vmem] * 2,
-        out_specs=vmem,
+        out_shape=[jax.ShapeDtypeStruct((OUTS, 4 * S), BF16), jax.ShapeDtypeStruct((R, C), F32)],
+        in_specs=[pl.BlockSpec(memory_space=pltpu.SMEM), vmem, vmem],
+        out_specs=[vmem, vmem],
         compiler_params=params,
-    )(raw, loss)
+    )(active, raw, loss)
     coef = pltpu.VMEM((5, R + 16, C), F32)
     half = jax.ShapeDtypeStruct((H, S, C), F32)
     conc, saved = pl.pallas_call(
         near_kernel,
         out_shape=[half, jax.ShapeDtypeStruct((SAVED, S, C), F32)],
-        in_specs=[smem] + [vmem] * 4,
+        in_specs=[vmem] * 5,
         out_specs=[vmem] * 2,
         scratch_shapes=[coef, pltpu.VMEM((5, FAR_FIRST + SUBS - 1, 8, C), F32)],
         compiler_params=params,
-    )(active, x, winds, from_near, w)
+    )(scale, x, winds, from_near, w)
     return pl.pallas_call(
         rest_kernel,
         out_shape=[jax.ShapeDtypeStruct((S, R, C), F32), jax.ShapeDtypeStruct((2, R, C), F32)],
-        in_specs=[smem] + [vmem] * 8,
+        in_specs=[vmem] * 8,
         out_specs=[hbm, vmem],
         scratch_shapes=[
             coef,
             pltpu.VMEM((5, H + SUBS - 2, 8, C), F32),
             pltpu.VMEM((H, S, C), F32),
             pltpu.VMEM((2, S, H, C), F32),
-            pltpu.SemaphoreType.DMA((2,)),
+            pltpu.SemaphoreType.DMA((2, S // B)),
         ],
         compiler_params=params,
-    )(active, x, winds, from_near, from_late, from_far, w, conc, saved)
+    )(scale, x, winds, from_near, from_far, w, conc, saved)
 
 
 def solution(mesh):

time: 26.7 us -> 23.7 us (0.89)
  starting transfers between devices: 12.3 us -> 9.07 us
  Pallas kernels: 12.7 us -> 13.2 us
    ppermute x1 -> x0, starting transfers between devices: 8.45 us -> none  [on_device(): from_late = lax.ppermute(to_far, AXES, late)]
    ppermute x1, starting transfers between devices: 1.28 us -> 6.52 us  [on_device(): from_far = lax.ppermute(to_far, AXES, far)]
    pallas_call x1, Pallas kernels: 4.21 us -> 5.43 us  [on_device(): pl.pallas_call(near_kernel, out_shape=[half, jax.ShapeDtypeStruct((SAVED,...]
    pallas_call x1, Pallas kernels: 6.93 us -> 6.17 us  [on_device(): pl.pallas_call(rest_kernel, out_shape=[jax.ShapeDtypeStruct((S, R, C), F3...]
  transfers between devices with their start and end apart: 3 -> 2, of which waited for: 0 -> 0; matrix products, arithmetic and copies ran while one was open for 0% -> 0% of each run, Pallas kernels for 17% -> 24%
where the time goes in v5:
time: 23.7 us; the launch traced here: 23.6 us
  Pallas kernels  13.2 us (56%)
  starting transfers between devices  9.07 us (38%)
  between operations  1.32 us (6%)
    ppermute x1, starting transfers between devices, on_device(): from_far = lax.ppermute(to_far, AXES, far)  6.52 us
    pallas_call x1, Pallas kernels, on_device(): pl.pallas_call(rest_kernel, out_shape=[jax.ShapeDtypeStruct((S, R, C), F3...  6.17 us
    pallas_call x1, Pallas kernels, on_device(): pl.pallas_call(near_kernel, out_shape=[half, jax.ShapeDtypeStruct((SAVED,...  5.43 us
    ppermute x1, starting transfers between devices, on_device(): from_near = lax.ppermute(to_near, AXES, near)  2.55 us
    pallas_call x1, Pallas kernels, on_device(): pl.pallas_call(pack_kernel, out_shape=[message, message, jax.ShapeDtypeSt...  1.45 us
  transfers between devices with their start and end apart: 2, of which 0 were waited for; matrix products, arithmetic and copies ran while one was open for 0% of the time, Pallas kernels for 24%

profile of v5, /device:TPU:1, one launch (start us, length us, event | category | flops | bytes accessed | tf_op | source)
XLA Modules:
  0.0 23.6 jit_solution(6293475775569699861)
XLA Ops:
  0.6 1.4 %shard_map.86 = (f32[528,128]{1,0:T(8,128)S(1)}, f32[528,128]{1,0:T(8,128)S(1)}, f32[2048,128]{1,0:T(8,128)S(1)}, f32[2,16,128]{2,1,0:T(8,128)S(1)}, f32[9,128,128]{2,1,0:T(8,128)S(1)}, /*index=5*/f32[1,128]{1,0:T(1,128)S(1)}) custom-call(f32[2048,128]{1,0:T(8,128)} %bitcast.2, f32[2,16,128]{2,1,0:T(8,128)} %winds_hbm.1, f32[128,128]{1,0:T(8,128)} %linear_hbm.1, ...), custom_call_target="tpu_custom_call" | custom-call | tf_op jit(solution)/shard_map/pallas_call | solution.py:303
  2.1 2.6 %collective-permute-start = (f32[528,128]{1,0:T(8,128)S(1)}, f32[528,128]{1,0:T(8,128)S(1)}, u32[]{:S(2)}, u32[]{:S(2)}) collective-permute-start(f32[528,128]{1,0:T(8,128)S(1)} %get-tuple-element.17), channel_id=1, source_target_pairs={{0,1},{1,0},{2,3},{3,2},{4,5},{5,4},{6,7},{7,6},{8,9},{9,8},{10,11... | collective-permute-start | bytes 811016 | tf_op jit(solution)/shard_map/ppermute | solution.py:323
  4.6 6.5 %collective-permute-start.1 = (f32[528,128]{1,0:T(8,128)S(1)}, f32[528,128]{1,0:T(8,128)S(1)}, u32[]{:S(2)}, u32[]{:S(2)}) collective-permute-start(f32[528,128]{1,0:T(8,128)S(1)} %get-tuple-element.18), channel_id=1, source_target_pairs={{0,255},{1,2},{2,1},{3,4},{4,3},{5,6},{6,5},{7,8},{8,7},{9,10},{10... | collective-permute-start | bytes 811016 | tf_op jit(solution)/shard_map/ppermute | solution.py:324
  11.8 0.2 shard_map.87
  12.0 0.0 collective-permute-done.near_ref
  12.0 5.4 %shard_map.88 = (f32[8,128,128]{2,1,0:T(8,128)S(1)}, f32[7,128,128]{2,1,0:T(8,128)S(1)}) custom-call(f32[16,128]{1,0:T(8,128)S(1)} %get-tuple-element.14.scale_ref, f32[2048,128]{1,0:T(8,128)S(1)} %get-tuple-element.15.x_ref, f32[2,16,128]{2,1,0:T(8,128)S(1)} %get-tuple-element.16.winds_ref, f32[528,128]{1,0:T(8,128)S(1)} %collective-permute-done.near_ref, ...), custom_call_target="tpu_custom_call" | custom-call | tf_op jit(solution)/shard_map/pallas_call | solution.py:334
  17.4 0.0 collective-permute-done.1.far_ref
  17.4 6.2 %shard_map.89 = (f32[128,16,128]{2,1,0:T(8,128)}, f32[2,16,128]{2,1,0:T(8,128)}) custom-call(f32[16,128]{1,0:T(8,128)S(1)} %get-tuple-element.14.scale_ref, f32[2048,128]{1,0:T(8,128)S(1)} %get-tuple-element.15.x_ref, f32[2,16,128]{2,1,0:T(8,128)S(1)} %get-tuple-element.16.winds_ref, f32[528,128]{1,0:T(8,128)S(1)} %collective-permute-done.near_ref, ...), custom_call_target="tpu_custom_call" | custom-call | tf_op jit(solution)/shard_map/pallas_call | solution.py:342
Async XLA Ops:
  2.1 9.9 %collective-permute-start = (f32[528,128]{1,0:T(8,128)S(1)}, f32[528,128]{1,0:T(8,128)S(1)}, u32[]{:S(2)}, u32[]{:S(2)}) collective-permute-start(f32[528,128]{1,0:T(8,128)S(1)} %get-tuple-element.17), channel_id=1, source_target_pairs={{0,1},{1,0},{2,3},{3,2},{4,5},{5,4},{6,7},{7,6},{8,9},{9,8},{10,11... | collective-permute-start | bytes 811016 | tf_op jit(solution)/shard_map/ppermute | solution.py:323
  4.6 12.8 %collective-permute-start.1 = (f32[528,128]{1,0:T(8,128)S(1)}, f32[528,128]{1,0:T(8,128)S(1)}, u32[]{:S(2)}, u32[]{:S(2)}) collective-permute-start(f32[528,128]{1,0:T(8,128)S(1)} %get-tuple-element.18), channel_id=1, source_target_pairs={{0,255},{1,2},{2,1},{3,4},{4,3},{5,6},{6,5},{7,8},{8,7},{9,10},{10... | collective-permute-start | bytes 811016 | tf_op jit(solution)/shard_map/ppermute | solution.py:324

commit v6 on v5

--- a/solution.py
+++ b/solution.py
@@ -232,8 +232,12 @@
     for m in range(H):
         store(conc_ref, m, states[m])
     conc = whole(conc_ref, range(H))
-    for _ in range(NEAR_STEPS):
-        conc = react(conc, scale_of(scale_ref, range(H)), w_ref)
+    scale = scale_of(scale_ref, range(H))
+    for _ in range(CHEM_STEPS - 1):
+        conc = react(conc, scale, w_ref)
+    if EARLY:
+        early = react(conc[:, : EARLY * C], scale[:, : EARLY * C], w_ref)
+        conc = jnp.concatenate([early, conc[:, EARLY * C :]], axis=1)
     for m in range(H):
         conc_ref[m] = conc[:, m * C : (m + 1) * C]
 
@@ -274,9 +278,10 @@
     winds_out_ref[0] = u[8:24]
     winds_out_ref[1] = v[8:24]
     coefficients(u, v, coef_ref, wide_ref, range(FAR_FIRST - SUBS + 1, R + SUBS - 1))
-    conc = whole(near_conc_ref, range(H))
-    for step in range(NEAR_STEPS, CHEM_STEPS):
-        conc = react(conc, scale_of(scale_ref, range(H)), w_ref)
+    late = react(whole(near_conc_ref, range(EARLY, H)), scale_of(scale_ref, range(EARLY, H)), w_ref)
+    conc = late
+    if EARLY:
+        conc = jnp.concatenate([whole(near_conc_ref, range(EARLY)), late], axis=1)
     put([conc[c * B : (c + 1) * B] for c in range(S // B)], 0, is_even())
     far_transport(x_ref, far_ref, saved_ref, wide_ref, conc_ref)
     conc = whole(conc_ref, range(H))
@@ -288,7 +293,7 @@
         copy.wait()
 
 
-NEAR_STEPS = 3
+EARLY = 4
 
 
 def on_device(tracers, winds, linear, loss, left, right, active):

time: 23.7 us -> 23.8 us (level)
  waiting for transfers between devices: 0.01 us -> 0.56 us
  Pallas kernels: 13.2 us -> 12.7 us
    pallas_call x1, Pallas kernels: 5.43 us -> 4.81 us  [on_device(): pl.pallas_call(near_kernel, out_shape=[half, jax.ShapeDtypeStruct((SAVED,...]
    ppermute x1, waiting for transfers between devices: 0.01 us -> 0.55 us  [on_device(): from_far = lax.ppermute(to_far, AXES, far)]
  transfers between devices with their start and end apart: 2 -> 2, of which waited for: 0 -> 1; matrix products, arithmetic and copies ran while one was open for 0% -> 0% of each run, Pallas kernels for 24% -> 21%
where the time goes in v6:
time: 23.8 us; the launch traced here: 23.6 us
  Pallas kernels  12.7 us (53%)
  starting transfers between devices  9.07 us (38%)
  between operations  1.32 us (6%)
  waiting for transfers between devices  0.56 us (2%)
    ppermute x1, starting transfers between devices, on_device(): from_far = lax.ppermute(to_far, AXES, far)  6.52 us
    pallas_call x1, Pallas kernels, on_device(): pl.pallas_call(rest_kernel, out_shape=[jax.ShapeDtypeStruct((S, R, C), F3...  6.28 us
    pallas_call x1, Pallas kernels, on_device(): pl.pallas_call(near_kernel, out_shape=[half, jax.ShapeDtypeStruct((SAVED,...  4.81 us
    ppermute x1, starting transfers between devices, on_device(): from_near = lax.ppermute(to_near, AXES, near)  2.55 us
    pallas_call x1, Pallas kernels, on_device(): pl.pallas_call(pack_kernel, out_shape=[message, message, jax.ShapeDtypeSt...  1.45 us
    ppermute x1, waiting for transfers between devices, on_device(): from_far = lax.ppermute(to_far, AXES, far)  0.55 us
  transfers between devices with their start and end apart: 2, of which 1 were waited for; matrix products, arithmetic and copies ran while one was open for 0% of the time, Pallas kernels for 21%

profile of v6, /device:TPU:1, one launch (start us, length us, event | category | flops | bytes accessed | tf_op | source)
XLA Modules:
  0.0 23.6 jit_solution(3287328173431145709)
XLA Ops:
  0.6 1.4 %shard_map.86 = (f32[528,128]{1,0:T(8,128)S(1)}, f32[528,128]{1,0:T(8,128)S(1)}, f32[2048,128]{1,0:T(8,128)S(1)}, f32[2,16,128]{2,1,0:T(8,128)S(1)}, f32[9,128,128]{2,1,0:T(8,128)S(1)}, /*index=5*/f32[1,128]{1,0:T(1,128)S(1)}) custom-call(f32[2048,128]{1,0:T(8,128)} %bitcast.2, f32[2,16,128]{2,1,0:T(8,128)} %winds_hbm.1, f32[128,128]{1,0:T(8,128)} %linear_hbm.1, ...), custom_call_target="tpu_custom_call" | custom-call | tf_op jit(solution)/shard_map/pallas_call | solution.py:308
  2.1 2.6 %collective-permute-start = (f32[528,128]{1,0:T(8,128)S(1)}, f32[528,128]{1,0:T(8,128)S(1)}, u32[]{:S(2)}, u32[]{:S(2)}) collective-permute-start(f32[528,128]{1,0:T(8,128)S(1)} %get-tuple-element.17), channel_id=1, source_target_pairs={{0,1},{1,0},{2,3},{3,2},{4,5},{5,4},{6,7},{7,6},{8,9},{9,8},{10,11... | collective-permute-start | bytes 811016 | tf_op jit(solution)/shard_map/ppermute | solution.py:328
  4.6 6.5 %collective-permute-start.1 = (f32[528,128]{1,0:T(8,128)S(1)}, f32[528,128]{1,0:T(8,128)S(1)}, u32[]{:S(2)}, u32[]{:S(2)}) collective-permute-start(f32[528,128]{1,0:T(8,128)S(1)} %get-tuple-element.18), channel_id=1, source_target_pairs={{0,255},{1,2},{2,1},{3,4},{4,3},{5,6},{6,5},{7,8},{8,7},{9,10},{10... | collective-permute-start | bytes 811016 | tf_op jit(solution)/shard_map/ppermute | solution.py:329
  11.8 0.2 shard_map.87
  12.0 0.0 collective-permute-done.near_ref
  12.0 4.8 %shard_map.88 = (f32[8,128,128]{2,1,0:T(8,128)S(1)}, f32[7,128,128]{2,1,0:T(8,128)S(1)}) custom-call(f32[16,128]{1,0:T(8,128)S(1)} %get-tuple-element.14.scale_ref, f32[2048,128]{1,0:T(8,128)S(1)} %get-tuple-element.15.x_ref, f32[2,16,128]{2,1,0:T(8,128)S(1)} %get-tuple-element.16.winds_ref, f32[528,128]{1,0:T(8,128)S(1)} %collective-permute-done.near_ref, ...), custom_call_target="tpu_custom_call" | custom-call | tf_op jit(solution)/shard_map/pallas_call | solution.py:339
  16.8 0.6 %collective-permute-done.1.far_ref = f32[528,128]{1,0:T(8,128)S(1)} collective-permute-done((f32[528,128]{1,0:T(8,128)S(1)}, f32[528,128]{1,0:T(8,128)S(1)}, u32[]{:S(2)}, u32[]{:S(2)}) %collective-permute-start.1) | collective-permute-done | bytes 270368 | tf_op jit(solution)/shard_map/ppermute | solution.py:329
  17.4 6.3 %shard_map.89 = (f32[128,16,128]{2,1,0:T(8,128)}, f32[2,16,128]{2,1,0:T(8,128)}) custom-call(f32[16,128]{1,0:T(8,128)S(1)} %get-tuple-element.14.scale_ref, f32[2048,128]{1,0:T(8,128)S(1)} %get-tuple-element.15.x_ref, f32[2,16,128]{2,1,0:T(8,128)S(1)} %get-tuple-element.16.winds_ref, f32[528,128]{1,0:T(8,128)S(1)} %collective-permute-done.near_ref, ...), custom_call_target="tpu_custom_call" | custom-call | tf_op jit(solution)/shard_map/pallas_call | solution.py:347
Async XLA Ops:
  2.1 9.9 %collective-permute-start = (f32[528,128]{1,0:T(8,128)S(1)}, f32[528,128]{1,0:T(8,128)S(1)}, u32[]{:S(2)}, u32[]{:S(2)}) collective-permute-start(f32[528,128]{1,0:T(8,128)S(1)} %get-tuple-element.17), channel_id=1, source_target_pairs={{0,1},{1,0},{2,3},{3,2},{4,5},{5,4},{6,7},{7,6},{8,9},{9,8},{10,11... | collective-permute-start | bytes 811016 | tf_op jit(solution)/shard_map/ppermute | solution.py:328
  4.6 12.7 %collective-permute-start.1 = (f32[528,128]{1,0:T(8,128)S(1)}, f32[528,128]{1,0:T(8,128)S(1)}, u32[]{:S(2)}, u32[]{:S(2)}) collective-permute-start(f32[528,128]{1,0:T(8,128)S(1)} %get-tuple-element.18), channel_id=1, source_target_pairs={{0,255},{1,2},{2,1},{3,4},{4,3},{5,6},{6,5},{7,8},{8,7},{9,10},{10... | collective-permute-start | bytes 811016 | tf_op jit(solution)/shard_map/ppermute | solution.py:329

commit v7 on v6

--- a/solution.py
+++ b/solution.py
@@ -36,8 +36,7 @@
 
 
 def pack_kernel(
-    x_hbm, winds_hbm, linear_hbm, loss_hbm, left_hbm, right_hbm,
-    near_ref, far_ref, x_ref, winds_ref, raw_ref, loss_ref, sems,
+    x_hbm, winds_hbm, near_ref, far_ref, x_ref, winds_ref, sems,
 ):
     even = is_even()
     moves = []
@@ -45,10 +44,6 @@
         part = pl.ds(k * (S * R // CHUNKS), S * R // CHUNKS)
         moves.append((x_hbm.at[part], x_ref.at[part]))
     moves.append((winds_hbm, winds_ref))
-    moves.append((left_hbm, raw_ref.at[pl.ds(1, PAIRS)]))
-    moves.append((right_hbm, raw_ref.at[pl.ds(1 + PAIRS, PAIRS)]))
-    moves.append((linear_hbm, raw_ref.at[0]))
-    moves.append((loss_hbm, loss_ref))
     copies = [pltpu.make_async_copy(a, b, sems.at[i]) for i, (a, b) in enumerate(moves)]
     for copy in copies:
         copy.start()
@@ -63,13 +58,9 @@
     for ref, side in ((near_ref, even), (far_ref, 1 - even)):
         for k in range(2):
             ref[pl.ds(SUBS * S + 8 * k, 8), :] = winds_ref[k, pl.ds(pl.multiple_of(side * 8, 8), 8), :]
-    for copy in copies[CHUNKS + 1 :]:
-        copy.wait()
-
-
-def weights_kernel(count_ref, raw_ref, loss_ref, w_ref, scale_ref):
-    cell = lax.broadcasted_iota(jnp.int32, (R, C), 0) * C + lax.broadcasted_iota(jnp.int32, (R, C), 1)
-    scale_ref[...] = jnp.where(cell < count_ref[0], DT_CHEM, 0.0).astype(F32)
+
+
+def join_weights(raw_ref, loss_ref, w_ref):
     row = lax.broadcasted_iota(jnp.int32, (S, S), 0)
     col = lax.broadcasted_iota(jnp.int32, (S, S), 1)
     diagonal = jnp.where(row == col, jnp.broadcast_to(loss_ref[...], (S, S)), 0.0)
@@ -193,8 +184,11 @@
 H = R // 2
 
 
-def scale_of(scale_ref, ms):
-    return jnp.concatenate([scale_ref[pl.ds(row_of(m), 1), :] for m in ms], axis=1)
+def scale_of(count_ref, ms):
+    col = lax.broadcasted_iota(jnp.int32, (1, C), 1)
+    return jnp.concatenate(
+        [jnp.where(col + row_of(m) * C < count_ref[0], DT_CHEM, 0.0).astype(F32) for m in ms], axis=1
+    )
 
 
 def whole(ref, slots):
@@ -217,7 +211,19 @@
 SAVED = 2 * (SUBS - 1) + 1
 
 
-def near_kernel(scale_ref, x_ref, winds_ref, near_ref, w_ref, conc_ref, saved_ref, coef_ref, wide_ref):
+def near_kernel(
+    count_ref, x_ref, winds_ref, near_ref, linear_hbm, loss_hbm, left_hbm, right_hbm,
+    conc_ref, saved_ref, w_ref, coef_ref, wide_ref, raw_ref, loss_ref, sems,
+):
+    moves = [
+        (left_hbm, raw_ref.at[pl.ds(1, PAIRS)]),
+        (right_hbm, raw_ref.at[pl.ds(1 + PAIRS, PAIRS)]),
+        (linear_hbm, raw_ref.at[0]),
+        (loss_hbm, loss_ref),
+    ]
+    copies = [pltpu.make_async_copy(a, b, sems.at[i]) for i, (a, b) in enumerate(moves)]
+    for copy in copies:
+        copy.start()
     u, v = new_winds(winds_ref, near_ref, near_ref)
     coefficients(u, v, coef_ref, wide_ref, range(1 - SUBS, FAR_FIRST))
     states = own_rows(x_ref, range(FAR_FIRST + 1)) | halo_rows(near_ref, range(-SUBS, 0), near_row)
@@ -231,8 +237,11 @@
             store(saved_ref, 2 * sub, states[last])
     for m in range(H):
         store(conc_ref, m, states[m])
+    for copy in copies:
+        copy.wait()
+    join_weights(raw_ref, loss_ref, w_ref)
     conc = whole(conc_ref, range(H))
-    scale = scale_of(scale_ref, range(H))
+    scale = scale_of(count_ref, range(H))
     for _ in range(CHEM_STEPS - 1):
         conc = react(conc, scale, w_ref)
     if EARLY:
@@ -256,7 +265,7 @@
 
 
 def rest_kernel(
-    scale_ref, x_ref, winds_ref, near_ref, far_ref, w_ref, near_conc_ref, saved_ref,
+    count_ref, x_ref, winds_ref, near_ref, far_ref, w_ref, near_conc_ref, saved_ref,
     out_hbm, winds_out_ref, coef_ref, wide_ref, conc_ref, stage_ref, sems,
 ):
     copies = []
@@ -278,14 +287,14 @@
     winds_out_ref[0] = u[8:24]
     winds_out_ref[1] = v[8:24]
     coefficients(u, v, coef_ref, wide_ref, range(FAR_FIRST - SUBS + 1, R + SUBS - 1))
-    late = react(whole(near_conc_ref, range(EARLY, H)), scale_of(scale_ref, range(EARLY, H)), w_ref)
+    late = react(whole(near_conc_ref, range(EARLY, H)), scale_of(count_ref, range(EARLY, H)), w_ref)
     conc = late
     if EARLY:
         conc = jnp.concatenate([whole(near_conc_ref, range(EARLY)), late], axis=1)
     put([conc[c * B : (c + 1) * B] for c in range(S // B)], 0, is_even())
     far_transport(x_ref, far_ref, saved_ref, wide_ref, conc_ref)
     conc = whole(conc_ref, range(H))
-    scale = scale_of(scale_ref, range(H, R))
+    scale = scale_of(count_ref, range(H, R))
     for step in range(CHEM_STEPS - 1):
         conc = react(conc, scale, w_ref)
     put(react_blocks(conc, scale, w_ref, True), 1, 1 - is_even())
@@ -293,7 +302,7 @@
         copy.wait()
 
 
-EARLY = 4
+EARLY = 6
 
 
 def on_device(tracers, winds, linear, loss, left, right, active):
@@ -305,49 +314,45 @@
     hbm = pl.BlockSpec(memory_space=pltpu.HBM)
     params = pltpu.CompilerParams(vmem_limit_bytes=VMEM_LIMIT)
     message = jax.ShapeDtypeStruct((SUBS * S + 16, C), F32)
-    to_near, to_far, x, winds, raw, loss = pl.pallas_call(
+    in_hbm = [
+        pltpu.with_memory_space_constraint(a, pltpu.HBM)
+        for a in (tracers.reshape(S * R, C), winds, linear, loss.reshape(1, S), left, right)
+    ]
+    to_near, to_far, x, winds = pl.pallas_call(
         pack_kernel,
-        out_shape=[
-            message,
-            message,
-            jax.ShapeDtypeStruct((S * R, C), F32),
-            jax.ShapeDtypeStruct((2, R, C), F32),
-            jax.ShapeDtypeStruct((1 + 2 * PAIRS, S, S), F32),
-            jax.ShapeDtypeStruct((1, S), F32),
-        ],
-        in_specs=[hbm] * 6,
-        out_specs=[vmem] * 6,
-        scratch_shapes=[pltpu.SemaphoreType.DMA((CHUNKS + 5,))],
+        out_shape=[message, message, jax.ShapeDtypeStruct((S * R, C), F32), jax.ShapeDtypeStruct((2, R, C), F32)],
+        in_specs=[hbm] * 2,
+        out_specs=[vmem] * 4,
+        scratch_shapes=[pltpu.SemaphoreType.DMA((CHUNKS + 1,))],
         compiler_params=params,
-    )(
-        *[
-            pltpu.with_memory_space_constraint(a, pltpu.HBM)
-            for a in (tracers.reshape(S * R, C), winds, linear, loss.reshape(1, S), left, right)
-        ]
-    )
+    )(*in_hbm[:2])
     from_near = lax.ppermute(to_near, AXES, near)
     from_far = lax.ppermute(to_far, AXES, far)
-    w, scale = pl.pallas_call(
-        weights_kernel,
-        out_shape=[jax.ShapeDtypeStruct((OUTS, 4 * S), BF16), jax.ShapeDtypeStruct((R, C), F32)],
-        in_specs=[pl.BlockSpec(memory_space=pltpu.SMEM), vmem, vmem],
-        out_specs=[vmem, vmem],
-        compiler_params=params,
-    )(active, raw, loss)
     coef = pltpu.VMEM((5, R + 16, C), F32)
     half = jax.ShapeDtypeStruct((H, S, C), F32)
-    conc, saved = pl.pallas_call(
+    smem = pl.BlockSpec(memory_space=pltpu.SMEM)
+    conc, saved, w = pl.pallas_call(
         near_kernel,
-        out_shape=[half, jax.ShapeDtypeStruct((SAVED, S, C), F32)],
-        in_specs=[vmem] * 5,
-        out_specs=[vmem] * 2,
-        scratch_shapes=[coef, pltpu.VMEM((5, FAR_FIRST + SUBS - 1, 8, C), F32)],
+        out_shape=[
+            half,
+            jax.ShapeDtypeStruct((SAVED, S, C), F32),
+            jax.ShapeDtypeStruct((OUTS, 4 * S), BF16),
+        ],
+        in_specs=[smem] + [vmem] * 3 + [hbm] * 4,
+        out_specs=[vmem] * 3,
+        scratch_shapes=[
+            coef,
+            pltpu.VMEM((5, FAR_FIRST + SUBS - 1, 8, C), F32),
+            pltpu.VMEM((1 + 2 * PAIRS, S, S), F32),
+            pltpu.VMEM((1, S), F32),
+            pltpu.SemaphoreType.DMA((4,)),
+        ],
         compiler_params=params,
-    )(scale, x, winds, from_near, w)
+    )(active, x, winds, from_near, *in_hbm[2:])
     return pl.pallas_call(
         rest_kernel,
         out_shape=[jax.ShapeDtypeStruct((S, R, C), F32), jax.ShapeDtypeStruct((2, R, C), F32)],
-        in_specs=[vmem] * 8,
+        in_specs=[smem] + [vmem] * 7,
         out_specs=[hbm, vmem],
         scratch_shapes=[
             coef,
@@ -357,7 +362,7 @@
             pltpu.SemaphoreType.DMA((2, S // B)),
         ],
         compiler_params=params,
-    )(scale, x, winds, from_near, from_far, w, conc, saved)
+    )(active, x, winds, from_near, from_far, w, conc, saved)
 
 
 def solution(mesh):

time: 23.8 us -> 24.5 us (1.029)
  Pallas kernels: 12.7 us -> 13.9 us
  waiting for transfers between devices: 0.56 us -> 0.01 us
    pallas_call x1, Pallas kernels: 4.81 us -> 6.41 us  [on_device(): pl.pallas_call(near_kernel, out_shape=[half, jax.ShapeDtypeStruct((SAVED,...]
    ppermute x1, waiting for transfers between devices: 0.55 us -> 0.01 us  [on_device(): from_far = lax.ppermute(to_far, AXES, far)]
  transfers between devices with their start and end apart: 2 -> 2, of which waited for: 1 -> 0; matrix products, arithmetic and copies ran while one was open for 0% -> 0% of each run, Pallas kernels for 21% -> 26%
where the time goes in v7:
time: 24.5 us; the launch traced here: 24.3 us
  Pallas kernels  13.9 us (57%)
  starting transfers between devices  9.07 us (37%)
  between operations  1.31 us (5%)
    ppermute x1, starting transfers between devices, on_device(): from_far = lax.ppermute(to_far, AXES, far)  6.52 us
    pallas_call x1, Pallas kernels, on_device(): pl.pallas_call(near_kernel, out_shape=[half, jax.ShapeDtypeStruct((SAVED,...  6.41 us
    pallas_call x1, Pallas kernels, on_device(): pl.pallas_call(rest_kernel, out_shape=[jax.ShapeDtypeStruct((S, R, C), F3...  6.25 us
    ppermute x1, starting transfers between devices, on_device(): from_near = lax.ppermute(to_near, AXES, near)  2.55 us
    pallas_call x1, Pallas kernels, on_device(): pl.pallas_call(pack_kernel, out_shape=[message, message, jax.ShapeDtypeSt...  1.28 us
  transfers between devices with their start and end apart: 2, of which 0 were waited for; matrix products, arithmetic and copies ran while one was open for 0% of the time, Pallas kernels for 26%

profile of v7, /device:TPU:1, one launch (start us, length us, event | category | flops | bytes accessed | tf_op | source)
XLA Modules:
  0.0 24.3 jit_solution(385578702446953127)
XLA Ops:
  0.6 1.3 %shard_map.86 = (f32[528,128]{1,0:T(8,128)S(1)}, f32[528,128]{1,0:T(8,128)S(1)}, f32[2048,128]{1,0:T(8,128)S(1)}, f32[2,16,128]{2,1,0:T(8,128)S(1)}) custom-call(f32[2048,128]{1,0:T(8,128)} %bitcast.2, f32[2,16,128]{2,1,0:T(8,128)} %winds_hbm.1), custom_call_target="tpu_custom_call" | custom-call | tf_op jit(solution)/shard_map/pallas_call | solution.py:321
  1.9 2.6 %collective-permute-start = (f32[528,128]{1,0:T(8,128)S(1)}, f32[528,128]{1,0:T(8,128)S(1)}, u32[]{:S(2)}, u32[]{:S(2)}) collective-permute-start(f32[528,128]{1,0:T(8,128)S(1)} %get-tuple-element.11), channel_id=1, source_target_pairs={{0,1},{1,0},{2,3},{3,2},{4,5},{5,4},{6,7},{7,6},{8,9},{9,8},{10,11... | collective-permute-start | bytes 811016 | tf_op jit(solution)/shard_map/ppermute | solution.py:329
  4.5 6.5 %collective-permute-start.1 = (f32[528,128]{1,0:T(8,128)S(1)}, f32[528,128]{1,0:T(8,128)S(1)}, u32[]{:S(2)}, u32[]{:S(2)}) collective-permute-start(f32[528,128]{1,0:T(8,128)S(1)} %get-tuple-element.12), channel_id=1, source_target_pairs={{0,255},{1,2},{2,1},{3,4},{4,3},{5,6},{6,5},{7,8},{8,7},{9,10},{10... | collective-permute-start | bytes 811016 | tf_op jit(solution)/shard_map/ppermute | solution.py:330
  11.6 0.0 collective-permute-done.near_ref
  11.7 6.4 %shard_map.87 = (f32[8,128,128]{2,1,0:T(8,128)S(1)}, f32[7,128,128]{2,1,0:T(8,128)S(1)}, bf16[1152,512]{1,0:T(8,128)(2,1)S(1)}) custom-call(s32[1]{0:T(128)S(6)} %copy.9.count_ref, f32[2048,128]{1,0:T(8,128)S(1)} %get-tuple-element.9.x_ref, f32[2,16,128]{2,1,0:T(8,128)S(1)} %get-tuple-element.10.winds_ref, f32[528,128]{1,0:T(8,128)S(1)} %collective-permute-done.near_ref, ...), custom_call_target="tpu_custom_call" | custom-call | tf_op jit(solution)/shard_map/pallas_call | solution.py:334
  18.1 0.0 collective-permute-done.1.far_ref
  18.1 6.2 %shard_map.88 = (f32[128,16,128]{2,1,0:T(8,128)}, f32[2,16,128]{2,1,0:T(8,128)}) custom-call(s32[1]{0:T(128)S(6)} %copy.9.count_ref, f32[2048,128]{1,0:T(8,128)S(1)} %get-tuple-element.9.x_ref, f32[2,16,128]{2,1,0:T(8,128)S(1)} %get-tuple-element.10.winds_ref, f32[528,128]{1,0:T(8,128)S(1)} %collective-permute-done.near_ref, ...), custom_call_target="tpu_custom_call" | custom-call | tf_op jit(solution)/shard_map/pallas_call | solution.py:352
Async XLA Ops:
  1.9 9.7 %collective-permute-start = (f32[528,128]{1,0:T(8,128)S(1)}, f32[528,128]{1,0:T(8,128)S(1)}, u32[]{:S(2)}, u32[]{:S(2)}) collective-permute-start(f32[528,128]{1,0:T(8,128)S(1)} %get-tuple-element.11), channel_id=1, source_target_pairs={{0,1},{1,0},{2,3},{3,2},{4,5},{5,4},{6,7},{7,6},{8,9},{9,8},{10,11... | collective-permute-start | bytes 811016 | tf_op jit(solution)/shard_map/ppermute | solution.py:329
  4.5 13.6 %collective-permute-start.1 = (f32[528,128]{1,0:T(8,128)S(1)}, f32[528,128]{1,0:T(8,128)S(1)}, u32[]{:S(2)}, u32[]{:S(2)}) collective-permute-start(f32[528,128]{1,0:T(8,128)S(1)} %get-tuple-element.12), channel_id=1, source_target_pairs={{0,255},{1,2},{2,1},{3,4},{4,3},{5,6},{6,5},{7,8},{8,7},{9,10},{10... | collective-permute-start | bytes 811016 | tf_op jit(solution)/shard_map/ppermute | solution.py:330
